TPU v7x, 1024 devices: a whole 4x8x16 slice. The times are simulated.
1024 devices in a mesh: node: 128 (over z, x, core), local: 8 (over y).
Axes of the slice: x: 4, y: 8, z: 16, core: 2. Of those that a mesh axis runs over, the one named last changes fastest.
Arguments:
- hidden_in: bfloat16 [2048, 4096], P('node', 'local'), may hold values from -6 to 6
- grad_out: bfloat16 [2048, 4096], P('node', 'local'), may hold values from -0.59765625 to 0.59765625
- expert_ids: int32 [2048, 8], P('node'), may hold values from 0 to 127, as said below
- route_weights: float32 [2048, 8], P('node'), may hold values from 0.05 to 0.5
- gate_weight: bfloat16 [128, 4096, 1024], P('node', 'local'), may hold values from -0.09375 to 0.09375
- up_weight: bfloat16 [128, 4096, 1024], P('node', 'local'), may hold values from -0.09375 to 0.09375
- down_weight: bfloat16 [128, 1024, 4096], P('node', None, 'local'), may hold values from -0.1875 to 0.1875
Outputs:
- grad_in: bfloat16 [2048, 4096], P('node', 'local')
- grad_weights: bfloat16 [2048, 8], P('node')
Inputs may be any that keep to these rules, and one draw needn't show every extreme that they name: `expert_ids`: expert e is held by node e; the experts form 8 groups of 16 consecutive numbers. Each token names 8 distinct experts, two in each of 4 distinct groups, and one group is named by every token of the same node. Within one node's block of 16 tokens no expert is named more than 2 times, and some expert exactly 2 times.
All inputs are finite; a program needn't handle non-finite values.
Results may differ from a plain program's by a relative error of at most 0.012.
Values may be sent and summed in bfloat16 or wider, within the bound.
No kernel may reach another device: no remote copies, remote signals or barrier semaphores. Data moves between devices by JAX's collectives and lax.ppermute only.
A program may use at most 32 MiB of HBM per device.

v0:
```python
import jax
import jax.numpy as jnp
from jax import lax
from jax.sharding import PartitionSpec as P


def contract_last(left, right):
    return lax.dot_general(
        left, right, (((1,), (1,)), ((), ())), preferred_element_type=jnp.float32
    )


def local_slots(expert_ids):
    tok_count = expert_ids.shape[0]
    matches = expert_ids[:, :, None, None] == expert_ids[None, None, :, :]
    order = jnp.arange(tok_count, dtype=jnp.int32)
    earlier = order[None, None, :, None] < order[:, None, None, None]
    return jnp.sum((matches & earlier).astype(jnp.int32), axis=(2, 3))


def hidden_grads(gate_pre, up_pre, grad_act):
    sig = jax.nn.sigmoid(gate_pre)
    silu_val = gate_pre * sig
    act = silu_val * up_pre
    score = jnp.sum(act * grad_act, axis=1)
    grad_gate = (grad_act * up_pre * sig * (1.0 + gate_pre * (1.0 - sig))).astype(jnp.bfloat16)
    grad_up = (grad_act * silu_val).astype(jnp.bfloat16)
    return (grad_gate, grad_up, score)


def on_device(hidden_in, grad_out, expert_ids, route_weights, gate_weight, up_weight, down_weight):
    node_count = lax.axis_size("node")
    tok_count, feat_width = hidden_in.shape
    route_count = expert_ids.shape[1]
    group_count = min(8, node_count // 2)
    slot_cap = 2 * tok_count // (node_count // group_count)
    slot_total = node_count * slot_cap
    slot_index = expert_ids * slot_cap + local_slots(expert_ids)
    owners = jnp.arange(tok_count * route_count, dtype=jnp.int32) // route_count
    source = jnp.full((slot_total,), tok_count, jnp.int32).at[slot_index.reshape(-1)].set(owners)
    x_pad = jnp.concatenate([hidden_in, jnp.zeros((1, feat_width), hidden_in.dtype)], axis=0)
    y_pad = jnp.concatenate([grad_out, jnp.zeros((1, feat_width), grad_out.dtype)], axis=0)
    x_send = x_pad[source].reshape(node_count, slot_cap, feat_width)
    y_send = y_pad[source].reshape(node_count, slot_cap, feat_width)
    x_recv, y_recv = (
        lax.all_to_all(x_send, "node", split_axis=0, concat_axis=0, tiled=True),
        lax.all_to_all(y_send, "node", split_axis=0, concat_axis=0, tiled=True),
    )
    x_rows = x_recv.reshape(slot_total, feat_width)
    y_rows = y_recv.reshape(slot_total, feat_width)
    w_gate = gate_weight[0]
    w_up = up_weight[0]
    w_down = down_weight[0]
    gate_part = jnp.dot(x_rows, w_gate, preferred_element_type=jnp.float32)
    up_part = jnp.dot(x_rows, w_up, preferred_element_type=jnp.float32)
    act_part = contract_last(y_rows, w_down)
    gate_pre, up_pre, grad_act = (
        lax.psum_scatter(gate_part, "local", scatter_dimension=1, tiled=True),
        lax.psum_scatter(up_part, "local", scatter_dimension=1, tiled=True),
        lax.psum_scatter(act_part, "local", scatter_dimension=1, tiled=True),
    )
    grad_gate, grad_up, score_part = hidden_grads(gate_pre, up_pre, grad_act)
    route_scores = lax.psum(score_part, "local").astype(jnp.bfloat16)
    grad_rows = contract_last(
        lax.all_gather(grad_gate, "local", axis=1, tiled=True), w_gate
    ) + contract_last(lax.all_gather(grad_up, "local", axis=1, tiled=True), w_up)
    grad_back = grad_rows.astype(jnp.bfloat16).reshape(node_count, slot_cap, feat_width)
    score_back = route_scores.reshape(node_count, slot_cap)
    grad_home, score_home = (
        lax.all_to_all(grad_back, "node", split_axis=0, concat_axis=0, tiled=True),
        lax.all_to_all(score_back, "node", split_axis=0, concat_axis=0, tiled=True),
    )
    grad_flat = grad_home.reshape(slot_total, feat_width)
    picked = grad_flat[slot_index].astype(jnp.float32)
    grad_in = jnp.einsum("tk,tkd->td", route_weights, picked).astype(jnp.bfloat16)
    grad_weights = score_home.reshape(slot_total)[slot_index]
    return (grad_in, grad_weights)


def solution(mesh):
    return jax.shard_map(
        on_device,
        mesh=mesh,
        in_specs=(
            P("node", "local"),
            P("node", "local"),
            P("node", None),
            P("node", None),
            P("node", "local", None),
            P("node", "local", None),
            P("node", None, "local"),
        ),
        out_specs=(P("node", "local"), P("node", None)),
        check_vma=False,
    )
```

profile of v0, /device:TPU:7, one launch (start us, length us, event | category | flops | bytes accessed | tf_op | source)
XLA Modules:
  0.0 329.3 jit_solution(1482579169085050364)
XLA Ops:
  7.3 0.8 copy.25
  8.1 2.5 convert_reduce_fusion
  10.8 1.0 scatter_custom_fusion
  11.8 1.2 gather_fusion.1
  13.1 45.2 %all_to_all.25 = bf16[128,2,512]{2,1,0:T(2,128)(2,1)S(1)} all-to-all(bf16[128,2,512]{2,1,0:T(2,128)(2,1)S(1)} %reshape.81), channel_id=1, replica_groups=mesh['node'=128,'local'=8] {'node'}, dimensions={0} | all-to-all | bytes 524288 | tf_op jit(solution)/shard_map/all_to_all | solution.py:46
  58.3 1.4 fusion.6
  59.9 1.5 fusion.3
  62.1 1.2 gather_fusion
  63.2 0.8 reshape.79
  64.0 28.9 %all_to_all.26 = bf16[128,2,512]{2,1,0:T(2,128)(2,1)} all-to-all(bf16[128,2,512]{2,1,0:T(2,128)(2,1)} %reshape.79), channel_id=1, replica_groups=mesh['node'=128,'local'=8] {'node'}, dimensions={0} | all-to-all | bytes 524288 | tf_op jit(solution)/shard_map/all_to_all | solution.py:47
  92.9 1.1 reshape.80
  94.0 1.5 fusion.8
  95.5 46.7 %reduce-scatter.8.cloned.1.call-done = f32[256,128]{1,0:T(8,128)} async-done(((f32[256,1024]{1,0:T(8,128)}), f32[256,128]{1,0:T(8,128)}) %reduce-scatter.8.cloned.1.call-update) | async-done | bytes 131088 | tf_op jit(solution)/shard_map/reduce_scatter | solution.py:58
  142.2 49.1 %reduce-scatter.4.cloned.1.call-done = f32[256,128]{1,0:T(8,128)} async-done(((f32[256,1024]{1,0:T(8,128)}), f32[256,128]{1,0:T(8,128)}) %reduce-scatter.4.cloned.1.call-update) | async-done | bytes 131088 | tf_op jit(solution)/shard_map/reduce_scatter | solution.py:60
  191.3 1.2 multiply_reduce_fusion
  192.5 18.0 %all_gather.6 = bf16[256,1024]{1,0:T(8,128)(2,1)S(1)} all-gather(bf16[256,128]{1,0:T(8,128)(2,1)S(1)} %get-tuple-element.13), channel_id=1, replica_groups=mesh['node'=128,'local'=8] {'local'}, dimensions={1}, use_global_device_ids=true | all-gather | bytes 589824 | tf_op jit(solution)/shard_map/all_gather | solution.py:65
  211.0 19.5 %all_gather.7 = bf16[256,1024]{1,0:T(8,128)(2,1)S(1)} all-gather(bf16[256,128]{1,0:T(8,128)(2,1)S(1)} %get-tuple-element.14), channel_id=1, replica_groups=mesh['node'=128,'local'=8] {'local'}, dimensions={1}, use_global_device_ids=true | all-gather | bytes 589824 | tf_op jit(solution)/shard_map/all_gather | solution.py:66
  230.5 11.5 %psum.7 = bf16[256]{0:T(256)(128)(2,1)S(1)} all-reduce(f32[256]{0:T(256)S(1)} %get-tuple-element.12), channel_id=1, replica_groups=mesh['node'=128,'local'=8] {'local'}, use_global_device_ids=true, to_apply=%region_6.7 | all-reduce | flops 256 | bytes 1536 | tf_op jit(solution)/shard_map/psum | solution.py:63
  242.7 35.8 %all-to-all-start.3 = ((bf16[128,1,2]{2,1,0:T(2,128)(2,1)}), bf16[128,1,2]{2,1,0:T(2,128)(2,1)S(1)}, u32[]{:S(2)}, u32[]{:S(2)}) async-start(bf16[128,1,2]{2,1,0:T(2,128)(2,1)} %all_to_all.20), calls=%async_computation.6 | async-start | bytes 131072 | tf_op jit(solution)/shard_map/all_to_all | solution.py:71
  279.8 12.1 %all-to-all-done.3 = bf16[128,1,2]{2,1,0:T(2,128)(2,1)S(1)} async-done(((bf16[128,1,2]{2,1,0:T(2,128)(2,1)}), bf16[128,1,2]{2,1,0:T(2,128)(2,1)S(1)}, u32[]{:S(2)}, u32[]{:S(2)}) %all-to-all-start.3) | async-done | bytes 544 | tf_op jit(solution)/shard_map/all_to_all | solution.py:71
  292.0 7.1 %all-to-all-start.2 = ((bf16[128,2,512]{2,1,0:T(2,128)(2,1)}), bf16[128,2,512]{2,1,0:T(2,128)(2,1)S(1)}, u32[]{:S(2)}, u32[]{:S(2)}) async-start(bf16[128,2,512]{2,1,0:T(2,128)(2,1)} %reshape.83), calls=%async_computation.5 | async-start | bytes 524288 | tf_op jit(solution)/shard_map/all_to_all | solution.py:70
  300.2 1.2 gather_fusion.3
  302.2 18.8 %all-to-all-done.2 = bf16[128,2,512]{2,1,0:T(2,128)(2,1)S(1)} async-done(((bf16[128,2,512]{2,1,0:T(2,128)(2,1)}), bf16[128,2,512]{2,1,0:T(2,128)(2,1)S(1)}, u32[]{:S(2)}, u32[]{:S(2)}) %all-to-all-start.2) | async-done | bytes 262176 | tf_op jit(solution)/shard_map/all_to_all | solution.py:70
  321.1 0.8 gather_fusion.2
  (46 shorter events, 6.5 us)
Async XLA Ops:
  7.2 52.7 %copy-start = (bf16[1,512,1024]{2,1,0:T(8,128)(2,1)S(1)}, bf16[1,512,1024]{2,1,0:T(8,128)(2,1)}, u32[]{:S(2)}) copy-start(bf16[1,512,1024]{2,1,0:T(8,128)(2,1)} %param.11) | copy-start | bytes 3145732
  7.2 88.3 %reduce-scatter.6.cloned.1.call-start = ((), (), s32[]{:S(2)}) async-start(), calls=%async_computation.8 | async-start | bytes 1179648 | tf_op jit(solution)/shard_map/reduce_scatter | solution.py:59
  7.2 0.9 copy-start.3
  10.7 1.1 copy-start.4
  13.0 45.4 %copy-start.1 = (bf16[1,512,1024]{2,1,0:T(8,128)(2,1)S(1)}, bf16[1,512,1024]{2,1,0:T(8,128)(2,1)}, u32[]{:S(2)}) copy-start(bf16[1,512,1024]{2,1,0:T(8,128)(2,1)} %param.12) | copy-start | bytes 3145732
  59.8 82.4 %reduce-scatter.8.cloned.1.call-start = ((), (), s32[]{:S(2)}) async-start(), calls=%async_computation.9 | async-start | bytes 1179648 | tf_op jit(solution)/shard_map/reduce_scatter | solution.py:58
  61.3 0.7 copy-start.5
  61.4 129.9 %reduce-scatter.4.cloned.1.call-start = ((), (), s32[]{:S(2)}) async-start(), calls=%async_computation.7 | async-start | bytes 1179648 | tf_op jit(solution)/shard_map/reduce_scatter | solution.py:60
  63.2 30.8 %copy-start.2 = (bf16[1,1024,512]{2,1,0:T(8,128)(2,1)S(1)}, bf16[1,1024,512]{2,1,0:T(8,128)(2,1)}, u32[]{:S(2)}) copy-start(bf16[1,1024,512]{2,1,0:T(8,128)(2,1)} %param.13) | copy-start | bytes 3145732
  242.7 49.2 %all-to-all-start.3 = ((bf16[128,1,2]{2,1,0:T(2,128)(2,1)}), bf16[128,1,2]{2,1,0:T(2,128)(2,1)S(1)}, u32[]{:S(2)}, u32[]{:S(2)}) async-start(bf16[128,1,2]{2,1,0:T(2,128)(2,1)} %all_to_all.20), calls=%async_computation.6 | async-start | bytes 131072 | tf_op jit(solution)/shard_map/all_to_all | solution.py:71
  292.0 29.1 %all-to-all-start.2 = ((bf16[128,2,512]{2,1,0:T(2,128)(2,1)}), bf16[128,2,512]{2,1,0:T(2,128)(2,1)S(1)}, u32[]{:S(2)}, u32[]{:S(2)}) async-start(bf16[128,2,512]{2,1,0:T(2,128)(2,1)} %reshape.83), calls=%async_computation.5 | async-start | bytes 524288 | tf_op jit(solution)/shard_map/all_to_all | solution.py:70
  299.1 0.7 copy-start.6
Sparse Core Ops, SparseCore 0:
  59.9 33.8 reduce-scatter.5
  97.3 44.8 reduce-scatter.7
  145.6 45.6 reduce-scatter.3
where the time goes:
time: 330 us; the launch traced here: 329 us
  waiting for transfers between devices  127 us (38%)
  blocking collectives  123 us (37%)
  starting transfers between devices  43.1 us (13%)
  between operations  14 us (4%)
  local copies, waits for them, and re-layouts  13 us (4%)
  matrix products  5.48 us (2%)
  other arithmetic  3.96 us (1%)
    reduce_scatter x1, waiting for transfers between devices, on_device(): lax.psum_scatter(act_part, 'local', scatter_dimension=1, tiled=True)  49.1 us
    reduce_scatter x1, waiting for transfers between devices, on_device(): lax.psum_scatter(gate_part, 'local', scatter_dimension=1, tiled=True)  46.7 us
    all_to_all x1, blocking collectives, on_device(): lax.all_to_all(x_send, 'node', split_axis=0, concat_axis=0, tiled=True)  45.2 us
    all_to_all x1, starting transfers between devices, on_device(): lax.all_to_all(score_back, 'node', split_axis=0, concat_axis=0, tiled=True)  35.8 us
    all_to_all x1, blocking collectives, on_device(): lax.all_to_all(y_send, 'node', split_axis=0, concat_axis=0, tiled=True)  28.9 us
    all_gather x1, blocking collectives, on_device(): lax.all_gather(grad_up, 'local', axis=1, tiled=True)  19.5 us
    all_to_all x1, waiting for transfers between devices, on_device(): lax.all_to_all(grad_back, 'node', split_axis=0, concat_axis=0, tiled=True)  18.8 us
    all_gather x1, blocking collectives, on_device(): lax.all_gather(grad_gate, 'local', axis=1, tiled=True)  18 us
  transfers between devices with their start and end apart: 5, of which 4 were waited for; matrix products, arithmetic and copies ran while one was open for 3% of the time, Pallas kernels for 0%

commit v1 on v0

v1 whole, which is shorter than its diff:
```python
import functools

import jax
import jax.numpy as jnp
from jax import lax
from jax.experimental import pallas as pl
from jax.experimental.pallas import tpu as pltpu
from jax.sharding import PartitionSpec as P

BF16 = jnp.bfloat16
F32 = jnp.float32
EMPTY = 64.0
LANES = 128
EXTRA = 16
PARAMS = pltpu.CompilerParams(vmem_limit_bytes=32 * 1024 * 1024)


def dot(left, right, left_dim=1, right_dim=0):
    return lax.dot_general(
        left, right, (((left_dim,), (right_dim,)), ((), ())), preferred_element_type=F32
    )


def iota(shape, dim):
    return lax.broadcasted_iota(jnp.int32, shape, dim)


def route_hits(ids, node_count, slot_cap):
    toks, routes = ids.shape
    experts = iota((toks, node_count), 1)
    named = jnp.zeros((toks, node_count), F32)
    for k in range(routes):
        named += (ids[:, k : k + 1] == experts).astype(F32)
    before = (iota((toks, toks), 1) < iota((toks, toks), 0)).astype(BF16)
    earlier = dot(before, named.astype(BF16))
    slots = iota((toks, node_count * slot_cap), 1)
    hits = []
    for k in range(routes):
        expert = ids[:, k : k + 1]
        slot = jnp.sum(jnp.where(expert == experts, earlier, 0.0), axis=1, keepdims=True)
        hits.append(slots == expert * slot_cap + slot.astype(jnp.int32))
    return hits


def dispatch_kernel(node_count, slot_cap, ids_ref, x_ref, y_ref, out_ref):
    toks = ids_ref.shape[0]
    hits = route_hits(ids_ref[...], node_count, slot_cap)
    taken = functools.reduce(jnp.logical_or, hits).astype(F32)
    free = 1.0 - jnp.sum(taken, axis=0, keepdims=True)
    free = jnp.where(iota(taken.shape, 0) == 0, jnp.broadcast_to(free, taken.shape), 0.0)
    pick = jnp.concatenate([taken, free], axis=0).astype(BF16)
    width = x_ref.shape[1]
    for place, ref in enumerate((x_ref, y_ref)):
        rows = jnp.concatenate([ref[...], jnp.full((toks, width), EMPTY, BF16)], axis=0)
        out_ref[:, place * width : (place + 1) * width] = dot(pick, rows, 0, 0).astype(BF16)


def parts_kernel(rows_ref, gate_ref, up_ref, down_ref, out_ref):
    parts = out_ref.shape[0]
    width = gate_ref.shape[0]
    x = rows_ref[:, :width]
    y = rows_ref[:, width:]
    for j in range(0, parts, 2):
        step = min(2, parts - j)
        cols = slice(j * LANES, (j + step) * LANES)
        products = (
            dot(x, gate_ref[:, cols]),
            dot(x, up_ref[:, cols]),
            dot(y, down_ref[cols, :], 1, 1),
        )
        for i in range(step):
            for place, value in enumerate(products):
                out_ref[j + i, :, place * LANES : (place + 1) * LANES] = value[
                    :, i * LANES : (i + 1) * LANES
                ].astype(BF16)


def hidden_kernel(parts_ref, out_ref):
    parts, rows, _ = parts_ref.shape
    total = parts_ref[0].astype(F32)
    for j in range(1, parts):
        total += parts_ref[j].astype(F32)
    gate_pre = total[:, :LANES]
    up_pre = total[:, LANES : 2 * LANES]
    grad_act = total[:, 2 * LANES :]
    sig = jax.nn.sigmoid(gate_pre)
    silu_val = gate_pre * sig
    product = silu_val * up_pre * grad_act
    grad_gate = (grad_act * up_pre * sig * (1.0 + gate_pre * (1.0 - sig))).astype(BF16)
    grad_up = (grad_act * silu_val).astype(BF16)
    score = lax.dot_general(
        jnp.ones((8, LANES), F32), product, (((1,), (1,)), ((), ())),
        preferred_element_type=F32, precision=lax.Precision.HIGHEST,
    )
    high = score.astype(BF16).astype(F32)
    tail = jnp.concatenate([high, score - high], axis=0).astype(BF16)
    pad = jnp.zeros((EXTRA, 2 * LANES - rows), BF16) if rows < 2 * LANES else None
    if pad is not None:
        tail = jnp.concatenate([tail, pad], axis=1)
    for j in range(parts):
        out_ref[j, :rows, :LANES] = grad_gate
        out_ref[j, :rows, LANES:] = grad_up
        out_ref[j, rows:, :] = tail


def back_kernel(hidden_ref, gate_ref, up_ref, out_ref):
    parts, rows, _ = hidden_ref.shape
    rows -= EXTRA
    width = gate_ref.shape[0]
    total = jnp.zeros((rows, width), F32)
    score = jnp.zeros((8, 2 * LANES), F32)
    for j in range(parts):
        cols = slice(j * LANES, (j + 1) * LANES)
        weights = jnp.concatenate([gate_ref[:, cols], up_ref[:, cols]], axis=1)
        total += dot(hidden_ref[j, :rows, :], weights, 1, 1)
        tail = hidden_ref[j, rows:, :].astype(F32)
        score += tail[:8] + tail[8:]
    out_ref[:, :width] = total.astype(BF16)
    score = score[:, :rows].astype(BF16)
    unit = (iota((rows, rows), 0) == iota((rows, rows), 1)).astype(BF16)
    spread = jnp.concatenate([score] * (LANES // 8), axis=0)
    out_ref[:, width:] = dot(unit, spread, 1, 1).astype(BF16)


def home_kernel(node_count, slot_cap, ids_ref, route_ref, back_ref, grad_ref, score_ref):
    width = grad_ref.shape[1]
    toks, routes = ids_ref.shape
    hits = route_hits(ids_ref[...], node_count, slot_cap)
    weight = jnp.zeros(hits[0].shape, F32)
    for k in range(routes):
        weight += jnp.where(hits[k], route_ref[:, k : k + 1], 0.0)
    high = weight.astype(BF16)
    rest = weight - high.astype(F32)
    middle = rest.astype(BF16)
    low = (rest - middle.astype(F32)).astype(BF16)
    split = jnp.concatenate([high, middle, low], axis=0)
    sums = dot(split, back_ref[:, :width])
    grad_ref[...] = (sums[:toks] + sums[toks : 2 * toks] + sums[2 * toks :]).astype(BF16)
    picks = jnp.concatenate([hit.astype(BF16) for hit in hits], axis=0)
    scores = dot(picks, back_ref[:, width:])
    lane = iota((toks, LANES), 1)
    placed = jnp.zeros((toks, LANES), F32)
    for k in range(routes):
        placed = jnp.where(lane == k, scores[k * toks : (k + 1) * toks], placed)
    score_ref[...] = placed[:, :routes].astype(BF16)


def on_device(hidden_in, grad_out, expert_ids, route_weights, gate_weight, up_weight, down_weight):
    node_count = lax.axis_size("node")
    parts = lax.axis_size("local")
    tok_count, width = hidden_in.shape
    group_count = min(8, node_count // 2)
    slot_cap = 2 * tok_count // (node_count // group_count)
    slot_total = node_count * slot_cap
    w_gate, w_up, w_down = gate_weight[0], up_weight[0], down_weight[0]

    def call(kernel, shape, *args):
        return pl.pallas_call(
            kernel,
            out_shape=jax.tree.map(lambda s: jax.ShapeDtypeStruct(s, BF16), shape, is_leaf=lambda s: isinstance(s, tuple) and isinstance(s[0], int)),
            compiler_params=PARAMS,
        )(*args)

    send = call(
        functools.partial(dispatch_kernel, node_count, slot_cap),
        (slot_total, 2 * width), expert_ids, hidden_in, grad_out,
    ).reshape(node_count, slot_cap, 2 * width)
    recv = lax.all_to_all(send, "node", split_axis=0, concat_axis=0, tiled=True)
    rows = recv.reshape(slot_total, 2 * width)
    sums = call(parts_kernel, (parts, slot_total, 3 * LANES), rows, w_gate, w_up, w_down)
    sums = lax.all_to_all(sums, "local", split_axis=0, concat_axis=0, tiled=True)
    hidden = call(hidden_kernel, (parts, slot_total + EXTRA, 2 * LANES), sums)
    hidden = lax.all_to_all(hidden, "local", split_axis=0, concat_axis=0, tiled=True)
    back = call(back_kernel, (slot_total, width + LANES), hidden, w_gate, w_up)
    back = back.reshape(node_count, slot_cap, width + LANES)
    home = lax.all_to_all(back, "node", split_axis=0, concat_axis=0, tiled=True)
    home = home.reshape(slot_total, width + LANES)
    grad_in, grad_weights = call(
        functools.partial(home_kernel, node_count, slot_cap),
        [(tok_count, width), (tok_count, expert_ids.shape[1])], expert_ids, route_weights, home,
    )
    return (grad_in, grad_weights)


def solution(mesh):
    return jax.shard_map(
        on_device,
        mesh=mesh,
        in_specs=(
            P("node", "local"),
            P("node", "local"),
            P("node", None),
            P("node", None),
            P("node", "local", None),
            P("node", "local", None),
            P("node", None, "local"),
        ),
        out_specs=(P("node", "local"), P("node", None)),
        check_vma=False,
    )
```

time: 330 us -> 180 us (0.55)
  waiting for transfers between devices: 127 us -> 24.7 us
  starting transfers between devices: 43.1 us -> 11.5 us
  between operations: 14 us -> 0.73 us
  blocking collectives: 123 us -> 132 us
  local copies, waits for them, and re-layouts: 13 us -> 6.56 us
  matrix products: 5.48 us -> 0 us
  Pallas kernels: 0 us -> 4.06 us
  other arithmetic: 3.96 us -> 0 us
    reduce_scatter x3 -> x0, waiting for transfers between devices: 95.8 us -> none  [the longest x1 49.1 us: on_device(): lax.psum_scatter(act_part, 'local', scatter_dimension=1, tiled=True)]
    all_to_all x2 -> x3, blocking collectives: 74 us -> 132 us  [the longest x1 56.3 us: on_device(): recv = lax.all_to_all(send, 'node', split_axis=0, concat_axis=0, tiled=True)]
    all_gather x2 -> x0, blocking collectives: 37.5 us -> none  [the longest x1 19.5 us: on_device(): lax.all_gather(grad_up, 'local', axis=1, tiled=True)]
    all_to_all x2 -> x1, starting transfers between devices: 42.9 us -> 11.5 us  [on_device(): home = lax.all_to_all(back, 'node', split_axis=0, concat_axis=0, tiled=True)]
    psum x1 -> x0, blocking collectives: 11.5 us -> none  [on_device(): route_scores = lax.psum(score_part, 'local').astype(jnp.bfloat16)]
    all_to_all x2 -> x1, waiting for transfers between devices: 30.9 us -> 24.7 us  [on_device(): home = lax.all_to_all(back, 'node', split_axis=0, concat_axis=0, tiled=True)]
    dot_general x6 -> x0, matrix products: 5.48 us -> none  [the longest x3 2.41 us: contract_last(): lax.dot_general(left, right, (((1,), (1,)), ((), ())), preferred_element_...]
    gather x5 -> x0, local copies, waits for them, and re-layouts: 4.47 us -> none  [the longest x2 1.32 us: on_device(): grad_weights = score_home.reshape(slot_total)[slot_index]]
  transfers between devices with their start and end apart: 5 -> 1, of which waited for: 4 -> 1; matrix products, arithmetic and copies ran while one was open for 3% -> 0% of each run, Pallas kernels for 0% -> 0%
where the time goes in v1:
time: 180 us; the launch traced here: 179 us
  blocking collectives  132 us (73%)
  waiting for transfers between devices  24.7 us (14%)
  starting transfers between devices  11.5 us (6%)
  local copies, waits for them, and re-layouts  6.56 us (4%)
  Pallas kernels  4.06 us (2%)
    all_to_all x1, blocking collectives, on_device(): recv = lax.all_to_all(send, 'node', split_axis=0, concat_axis=0, tiled=True)  56.3 us
    all_to_all x1, blocking collectives, on_device(): lax.all_to_all(sums, 'local', split_axis=0, concat_axis=0, tiled=True)  45.7 us
    all_to_all x1, blocking collectives, on_device(): lax.all_to_all(hidden, 'local', split_axis=0, concat_axis=0, tiled=True)  29.6 us
    all_to_all x1, waiting for transfers between devices, on_device(): home = lax.all_to_all(back, 'node', split_axis=0, concat_axis=0, tiled=True)  24.7 us
    all_to_all x1, starting transfers between devices, on_device(): home = lax.all_to_all(back, 'node', split_axis=0, concat_axis=0, tiled=True)  11.5 us
    pallas_call x5, Pallas kernels, call(): pl.pallas_call(kernel, out_shape=jax.tree.map(lambda s: jax.ShapeDtypeStr...  4.06 us
  transfers between devices with their start and end apart: 1, of which 1 were waited for; matrix products, arithmetic and copies ran while one was open for 0% of the time, Pallas kernels for 0%

profile of v1, /device:TPU:7, one launch (start us, length us, event | category | flops | bytes accessed | tf_op | source)
XLA Modules:
  0.0 179.2 jit_solution(3791125324298059569)
XLA Ops:
  0.6 0.8 copy.10.ids_ref
  1.4 0.7 copy-done.3
  2.1 0.7 copy-done.4
  2.8 0.7 shard_map.86
  3.5 0.0 copy-start
  3.5 0.0 copy-start.1
  3.6 0.2 reshape.16
  3.8 56.3 %all_to_all.20 = bf16[128,2,1024]{2,1,0:T(2,128)(2,1)} all-to-all(bf16[128,2,1024]{2,1,0:T(2,128)(2,1)S(1)} %reshape.16), channel_id=1, replica_groups=mesh['node'=128,'local'=8] {'node'}, dimensions={0} | all-to-all | bytes 1048576 | tf_op jit(solution)/shard_map/all_to_all | solution.py:168
  60.1 1.2 reshape.17.rows_ref
  61.3 0.0 copy-start.2
  61.4 1.2 copy-done.2
  62.6 1.0 shard_map.87
  63.6 45.7 %all_to_all.21.parts_ref = bf16[8,256,384]{2,1,0:T(8,128)(2,1)S(1)} all-to-all(bf16[8,256,384]{2,1,0:T(8,128)(2,1)S(1)} %shard_map.87), channel_id=1, replica_groups=mesh['node'=128,'local'=8] {'local'}, dimensions={0} | all-to-all | bytes 3145728 | tf_op jit(solution)/shard_map/all_to_all | solution.py:171
  109.3 0.4 shard_map.88
  109.7 29.6 %all_to_all.22.hidden_ref = bf16[8,272,256]{2,1,0:T(8,128)(2,1)S(1)} all-to-all(bf16[8,272,256]{2,1,0:T(8,128)(2,1)S(1)} %shard_map.88), channel_id=1, replica_groups=mesh['node'=128,'local'=8] {'local'}, dimensions={0} | all-to-all | bytes 2228224 | tf_op jit(solution)/shard_map/all_to_all | solution.py:173
  139.3 0.8 shard_map.89
  140.1 0.8 reshape.18
  140.9 11.5 %all-to-all-start.3 = ((bf16[128,2,640]{2,1,0:T(2,128)(2,1)}), bf16[128,2,640]{2,1,0:T(2,128)(2,1)S(1)}, u32[]{:S(2)}, u32[]{:S(2)}) async-start(bf16[128,2,640]{2,1,0:T(2,128)(2,1)} %reshape.18), calls=%async_computation.3 | async-start | bytes 655360 | tf_op jit(solution)/shard_map/all_to_all | solution.py:176
  152.4 0.0 copy-done.5
  152.5 0.1 copy.11.route_ref
  152.5 24.7 %all-to-all-done.3 = bf16[128,2,640]{2,1,0:T(2,128)(2,1)S(1)} async-done(((bf16[128,2,640]{2,1,0:T(2,128)(2,1)}), bf16[128,2,640]{2,1,0:T(2,128)(2,1)S(1)}, u32[]{:S(2)}, u32[]{:S(2)}) %all-to-all-start.3) | async-done | bytes 327712 | tf_op jit(solution)/shard_map/all_to_all | solution.py:176
  177.2 0.1 reshape.19.back_ref
  177.4 1.1 shard_map.90
  178.5 0.7 copy.12
  (5 shorter events, 0.0 us)
Async XLA Ops:
  1.4 0.7 copy-start.3
  2.1 0.7 copy-start.4
  3.5 57.8 %copy-start = (bf16[1,512,1024]{2,1,0:T(8,128)(2,1)S(1)}, bf16[1,512,1024]{2,1,0:T(8,128)(2,1)}, u32[]{:S(2)}) copy-start(bf16[1,512,1024]{2,1,0:T(8,128)(2,1)} %param.11) | copy-start | bytes 3145732
  3.5 57.8 %copy-start.1 = (bf16[1,512,1024]{2,1,0:T(8,128)(2,1)S(1)}, bf16[1,512,1024]{2,1,0:T(8,128)(2,1)}, u32[]{:S(2)}) copy-start(bf16[1,512,1024]{2,1,0:T(8,128)(2,1)} %param.12) | copy-start | bytes 3145732
  61.3 1.2 copy-start.2
  139.3 13.2 %copy-start.5 = (f32[16,8]{0,1:T(8,128)S(1)}, f32[16,8]{0,1:T(8,128)}, u32[]{:S(2)}) copy-start(f32[16,8]{0,1:T(8,128)} %param.10) | copy-start | bytes 1540
  140.9 36.3 %all-to-all-start.3 = ((bf16[128,2,640]{2,1,0:T(2,128)(2,1)}), bf16[128,2,640]{2,1,0:T(2,128)(2,1)S(1)}, u32[]{:S(2)}, u32[]{:S(2)}) async-start(bf16[128,2,640]{2,1,0:T(2,128)(2,1)} %reshape.18), calls=%async_computation.3 | async-start | bytes 655360 | tf_op jit(solution)/shard_map/all_to_all | solution.py:176

commit v2 on v1

--- a/solution.py
+++ b/solution.py
@@ -55,11 +55,19 @@
         out_ref[:, place * width : (place + 1) * width] = dot(pick, rows, 0, 0).astype(BF16)
 
 
-def parts_kernel(rows_ref, gate_ref, up_ref, down_ref, out_ref):
-    parts = out_ref.shape[0]
-    width = gate_ref.shape[0]
-    x = rows_ref[:, :width]
-    y = rows_ref[:, width:]
+def parts_kernel(rows_ref, gate_ref, up_ref, down_ref, main_ref, rest_ref, place_ref, count_ref):
+    parts, main, _ = main_ref.shape
+    slots = rows_ref.shape[0]
+    width = gate_ref.shape[0]
+    named = rows_ref[:, :LANES].astype(F32)[:, :1] < 0.5 * EMPTY
+    named_wide = jnp.broadcast_to(named.astype(F32), (slots, LANES))
+    before = (iota((slots, slots), 1) < iota((slots, slots), 0)).astype(BF16)
+    order = dot(before, named_wide.astype(BF16))[:, :1].astype(jnp.int32)
+    place = (jnp.where(named, order, slots) == iota((slots, slots), 1)).astype(BF16)
+    place_ref[...] = place
+    count_ref[0, 0] = jnp.sum(named_wide[:, :1]).astype(jnp.int32)
+    x = dot(place, rows_ref[:, :width], 0, 0).astype(BF16)
+    y = dot(place, rows_ref[:, width:], 0, 0).astype(BF16)
     for j in range(0, parts, 2):
         step = min(2, parts - j)
         cols = slice(j * LANES, (j + step) * LANES)
@@ -69,10 +77,10 @@
             dot(y, down_ref[cols, :], 1, 1),
         )
         for i in range(step):
-            for place, value in enumerate(products):
-                out_ref[j + i, :, place * LANES : (place + 1) * LANES] = value[
-                    :, i * LANES : (i + 1) * LANES
-                ].astype(BF16)
+            for at, value in enumerate(products):
+                piece = value[:, i * LANES : (i + 1) * LANES].astype(BF16)
+                main_ref[j + i, :, at * LANES : (at + 1) * LANES] = piece[:main]
+                rest_ref[j + i, :, at * LANES : (at + 1) * LANES] = piece[main:]
 
 
 def hidden_kernel(parts_ref, out_ref):
@@ -103,7 +111,7 @@
         out_ref[j, rows:, :] = tail
 
 
-def back_kernel(hidden_ref, gate_ref, up_ref, out_ref):
+def back_rows(hidden_ref, gate_ref, up_ref):
     parts, rows, _ = hidden_ref.shape
     rows -= EXTRA
     width = gate_ref.shape[0]
@@ -115,11 +123,24 @@
         total += dot(hidden_ref[j, :rows, :], weights, 1, 1)
         tail = hidden_ref[j, rows:, :].astype(F32)
         score += tail[:8] + tail[8:]
-    out_ref[:, :width] = total.astype(BF16)
-    score = score[:, :rows].astype(BF16)
-    unit = (iota((rows, rows), 0) == iota((rows, rows), 1)).astype(BF16)
+    score = score.astype(BF16)
+    unit = (iota((rows, 2 * LANES), 0) == iota((rows, 2 * LANES), 1)).astype(BF16)
     spread = jnp.concatenate([score] * (LANES // 8), axis=0)
-    out_ref[:, width:] = dot(unit, spread, 1, 1).astype(BF16)
+    return total.astype(BF16), dot(unit, spread, 1, 1).astype(BF16)
+
+
+def rest_kernel(hidden_ref, gate_ref, up_ref, out_ref):
+    width = gate_ref.shape[0]
+    out_ref[:, :width], out_ref[:, width:] = back_rows(hidden_ref, gate_ref, up_ref)
+
+
+def back_kernel(hidden_ref, gate_ref, up_ref, rest_ref, place_ref, out_ref):
+    width = gate_ref.shape[0]
+    main, main_score = back_rows(hidden_ref, gate_ref, up_ref)
+    rows = jnp.concatenate([main, rest_ref[:, :width]], axis=0)
+    out_ref[:, :width] = dot(place_ref[...], rows).astype(BF16)
+    score = jnp.concatenate([main_score, rest_ref[:, width:]], axis=0)
+    out_ref[:, width:] = dot(place_ref[...], score).astype(BF16)
 
 
 def home_kernel(node_count, slot_cap, ids_ref, route_ref, back_ref, grad_ref, score_ref):
@@ -167,11 +188,36 @@
     ).reshape(node_count, slot_cap, 2 * width)
     recv = lax.all_to_all(send, "node", split_axis=0, concat_axis=0, tiled=True)
     rows = recv.reshape(slot_total, 2 * width)
-    sums = call(parts_kernel, (parts, slot_total, 3 * LANES), rows, w_gate, w_up, w_down)
-    sums = lax.all_to_all(sums, "local", split_axis=0, concat_axis=0, tiled=True)
-    hidden = call(hidden_kernel, (parts, slot_total + EXTRA, 2 * LANES), sums)
-    hidden = lax.all_to_all(hidden, "local", split_axis=0, concat_axis=0, tiled=True)
-    back = call(back_kernel, (slot_total, width + LANES), hidden, w_gate, w_up)
+    main = max(EXTRA, slot_total * 5 // 8 // EXTRA * EXTRA)
+    vmem = pl.BlockSpec(memory_space=pltpu.VMEM)
+    main_sums, rest_sums, place, count = pl.pallas_call(
+        parts_kernel,
+        out_shape=[
+            jax.ShapeDtypeStruct((parts, main, 3 * LANES), BF16),
+            jax.ShapeDtypeStruct((parts, slot_total - main, 3 * LANES), BF16),
+            jax.ShapeDtypeStruct((slot_total, slot_total), BF16),
+            jax.ShapeDtypeStruct((1, 1), jnp.int32),
+        ],
+        out_specs=[vmem, vmem, vmem, pl.BlockSpec(memory_space=pltpu.SMEM)],
+        compiler_params=PARAMS,
+    )(rows, w_gate, w_up, w_down)
+
+    def over_local(sums):
+        sums = lax.all_to_all(sums, "local", split_axis=0, concat_axis=0, tiled=True)
+        hidden = call(hidden_kernel, (parts, sums.shape[1] + EXTRA, 2 * LANES), sums)
+        return lax.all_to_all(hidden, "local", split_axis=0, concat_axis=0, tiled=True)
+
+    def rest_of(sums, w_gate, w_up):
+        return call(rest_kernel, (slot_total - main, width + LANES), over_local(sums), w_gate, w_up)
+
+    rest = lax.cond(
+        count[0, 0] > main,
+        rest_of,
+        lambda *_: jnp.zeros((slot_total - main, width + LANES), BF16),
+        rest_sums, w_gate, w_up,
+    )
+    hidden = over_local(main_sums)
+    back = call(back_kernel, (slot_total, width + LANES), hidden, w_gate, w_up, rest, place)
     back = back.reshape(node_count, slot_cap, width + LANES)
     home = lax.all_to_all(back, "node", split_axis=0, concat_axis=0, tiled=True)
     home = home.reshape(slot_total, width + LANES)

time: 180 us -> 161 us (0.89)
  blocking collectives: 132 us -> 54.8 us
  waiting for transfers between devices: 24.7 us -> 57.6 us
  starting transfers between devices: 11.5 us -> 34.6 us
  Pallas kernels: 4.06 us -> 6.78 us
    all_to_all x3 -> x2, blocking collectives: 132 us -> 54.8 us  [the longest x1 33 us: over_local(): lax.all_to_all(sums, 'local', split_axis=0, concat_axis=0, tiled=True)]
    all_to_all x0 -> x1, waiting for transfers between devices: none -> 32.9 us  [on_device(): recv = lax.all_to_all(send, 'node', split_axis=0, concat_axis=0, tiled=True)]
    all_to_all x0 -> x1, starting transfers between devices: none -> 23.5 us  [on_device(): recv = lax.all_to_all(send, 'node', split_axis=0, concat_axis=0, tiled=True)]
    pallas_call x0 -> x1, Pallas kernels: none -> 3.45 us  [on_device(): pl.pallas_call(parts_kernel, out_shape=[jax.ShapeDtypeStruct((parts, main...]
    pallas_call x5 -> x4, Pallas kernels: 4.06 us -> 3.33 us  [call(): pl.pallas_call(kernel, out_shape=jax.tree.map(lambda s: jax.ShapeDtypeStr...]
  transfers between devices with their start and end apart: 1 -> 2, of which waited for: 1 -> 2; matrix products, arithmetic and copies ran while one was open for 0% -> 0% of each run, Pallas kernels for 0% -> 0%
where the time goes in v2:
time: 161 us; the launch traced here: 160 us
  waiting for transfers between devices  57.6 us (36%)
  blocking collectives  54.8 us (34%)
  starting transfers between devices  34.6 us (21%)
  Pallas kernels  6.78 us (4%)
  local copies, waits for them, and re-layouts  5.11 us (3%)
    all_to_all x1, blocking collectives, over_local(): lax.all_to_all(sums, 'local', split_axis=0, concat_axis=0, tiled=True)  33 us
    all_to_all x1, waiting for transfers between devices, on_device(): recv = lax.all_to_all(send, 'node', split_axis=0, concat_axis=0, tiled=True)  32.9 us
    all_to_all x1, waiting for transfers between devices, on_device(): home = lax.all_to_all(back, 'node', split_axis=0, concat_axis=0, tiled=True)  24.7 us
    all_to_all x1, starting transfers between devices, on_device(): recv = lax.all_to_all(send, 'node', split_axis=0, concat_axis=0, tiled=True)  23.5 us
    all_to_all x1, blocking collectives, over_local(): lax.all_to_all(hidden, 'local', split_axis=0, concat_axis=0, tiled=True)  21.8 us
    all_to_all x1, starting transfers between devices, on_device(): home = lax.all_to_all(back, 'node', split_axis=0, concat_axis=0, tiled=True)  11.1 us
    pallas_call x1, Pallas kernels, on_device(): pl.pallas_call(parts_kernel, out_shape=[jax.ShapeDtypeStruct((parts, main...  3.45 us
    pallas_call x4, Pallas kernels, call(): pl.pallas_call(kernel, out_shape=jax.tree.map(lambda s: jax.ShapeDtypeStr...  3.33 us
  transfers between devices with their start and end apart: 2, of which 2 were waited for; matrix products, arithmetic and copies ran while one was open for 0% of the time, Pallas kernels for 0%

profile of v2, /device:TPU:7, one launch (start us, length us, event | category | flops | bytes accessed | tf_op | source)
XLA Modules:
  0.0 160.4 jit_solution(8111713354411516483)
XLA Ops:
  0.6 0.8 copy.10.ids_ref
  1.4 0.7 copy-done.1
  2.1 0.7 copy-done.2
  2.8 0.7 shard_map.86
  3.5 1.0 reshape.20
  4.5 23.5 %all-to-all-start.2 = ((bf16[128,2,1024]{2,1,0:T(2,128)(2,1)}), bf16[128,2,1024]{2,1,0:T(2,128)(2,1)S(1)}, u32[]{:S(2)}, u32[]{:S(2)}) async-start(bf16[128,2,1024]{2,1,0:T(2,128)(2,1)} %reshape.20), calls=%async_computation.2 | async-start | bytes 1048576 | tf_op jit(solution)/shard_map/all_to_all | solution.py:189
  28.0 32.9 %all-to-all-done.2 = bf16[128,2,1024]{2,1,0:T(2,128)(2,1)S(1)} async-done(((bf16[128,2,1024]{2,1,0:T(2,128)(2,1)}), bf16[128,2,1024]{2,1,0:T(2,128)(2,1)S(1)}, u32[]{:S(2)}, u32[]{:S(2)}) %all-to-all-start.2) | async-done | bytes 524320 | tf_op jit(solution)/shard_map/all_to_all | solution.py:189
  60.9 0.2 reshape.21.rows_ref
  61.1 0.0 copy-done
  61.2 3.4 %shard_map.87 = (bf16[8,160,384]{2,1,0:T(8,128)(2,1)S(1)}, bf16[8,96,384]{2,1,0:T(8,128)(2,1)S(1)}, bf16[256,256]{1,0:T(8,128)(2,1)S(1)}, s32[1,1]{1,0:T(1,128)}) custom-call(bf16[256,1024]{1,0:T(8,128)(2,1)S(1)} %reshape.21.rows_ref, bf16[512,1024]{1,0:T(8,128)(2,1)} %bitcast.5, bf16[512,1024]{1,0:T(8,128)(2,1)} %bitcast.8, bf16[1024,512]{1,0:T(8,128)(2,1)S(1)} %bitcast.4), custom_call_target="tpu_custom_call" | custom-call | tf_op jit(solution)/shard_map/pallas_call | solution.py:193
  65.3 33.0 %all_to_all.30.parts_ref = bf16[8,160,384]{2,1,0:T(8,128)(2,1)S(1)} all-to-all(bf16[8,160,384]{2,1,0:T(8,128)(2,1)S(1)} %get-tuple-element.18), channel_id=1, replica_groups=mesh['node'=128,'local'=8] {'local'}, dimensions={0} | all-to-all | bytes 1966080 | tf_op jit(solution)/shard_map/all_to_all | solution.py:206
  98.3 0.4 shard_map.88
  98.7 0.0 copy-start.3
  98.7 21.8 %all_to_all.31.hidden_ref = bf16[8,176,256]{2,1,0:T(8,128)(2,1)S(1)} all-to-all(bf16[8,176,256]{2,1,0:T(8,128)(2,1)S(1)} %shard_map.88), channel_id=1, replica_groups=mesh['node'=128,'local'=8] {'local'}, dimensions={0} | all-to-all | bytes 1441792 | tf_op jit(solution)/shard_map/all_to_all | solution.py:208
  120.5 0.0 copy-done.5
  120.5 0.0 copy-done.3
  120.5 1.1 shard_map.89
  121.7 0.8 reshape.22
  122.5 11.1 %all-to-all-start.5 = ((bf16[128,2,640]{2,1,0:T(2,128)(2,1)}), bf16[128,2,640]{2,1,0:T(2,128)(2,1)S(1)}, u32[]{:S(2)}, u32[]{:S(2)}) async-start(bf16[128,2,640]{2,1,0:T(2,128)(2,1)} %reshape.22), calls=%async_computation.5 | async-start | bytes 655360 | tf_op jit(solution)/shard_map/all_to_all | solution.py:222
  133.7 0.1 copy.11.route_ref
  133.7 24.7 %all-to-all-done.5 = bf16[128,2,640]{2,1,0:T(2,128)(2,1)S(1)} async-done(((bf16[128,2,640]{2,1,0:T(2,128)(2,1)}), bf16[128,2,640]{2,1,0:T(2,128)(2,1)S(1)}, u32[]{:S(2)}, u32[]{:S(2)}) %all-to-all-start.5) | async-done | bytes 327712 | tf_op jit(solution)/shard_map/all_to_all | solution.py:222
  158.5 0.1 reshape.23.back_ref
  158.6 1.1 shard_map.90
  159.7 0.7 copy.12
  (8 shorter events, 0.1 us)
Async XLA Ops:
  1.4 0.7 copy-start.1
  2.1 0.7 copy-start.2
  4.5 56.6 %copy-start = (bf16[1,1024,512]{2,1,0:T(8,128)(2,1)S(1)}, bf16[1,1024,512]{2,1,0:T(8,128)(2,1)}, u32[]{:S(2)}) copy-start(bf16[1,1024,512]{2,1,0:T(8,128)(2,1)} %param.15) | copy-start | bytes 3145732
  4.5 56.4 %all-to-all-start.2 = ((bf16[128,2,1024]{2,1,0:T(2,128)(2,1)}), bf16[128,2,1024]{2,1,0:T(2,128)(2,1)S(1)}, u32[]{:S(2)}, u32[]{:S(2)}) async-start(bf16[128,2,1024]{2,1,0:T(2,128)(2,1)} %reshape.20), calls=%async_computation.2 | async-start | bytes 1048576 | tf_op jit(solution)/shard_map/all_to_all | solution.py:189
  98.3 22.2 %copy-start.5 = (bf16[1,512,1024]{2,1,0:T(8,128)(2,1)S(1)}, bf16[1,512,1024]{2,1,0:T(8,128)(2,1)}, u32[]{:S(2)}) copy-start(bf16[1,512,1024]{2,1,0:T(8,128)(2,1)} %param.14) | copy-start | bytes 3145732
  98.7 21.8 %copy-start.3 = (bf16[1,512,1024]{2,1,0:T(8,128)(2,1)S(1)}, bf16[1,512,1024]{2,1,0:T(8,128)(2,1)}, u32[]{:S(2)}) copy-start(bf16[1,512,1024]{2,1,0:T(8,128)(2,1)} %param.13) | copy-start | bytes 3145732
  122.5 11.2 %copy-start.7 = (f32[16,8]{0,1:T(8,128)S(1)}, f32[16,8]{0,1:T(8,128)}, u32[]{:S(2)}) copy-start(f32[16,8]{0,1:T(8,128)} %param.12) | copy-start | bytes 1540
  122.5 35.9 %all-to-all-start.5 = ((bf16[128,2,640]{2,1,0:T(2,128)(2,1)}), bf16[128,2,640]{2,1,0:T(2,128)(2,1)S(1)}, u32[]{:S(2)}, u32[]{:S(2)}) async-start(bf16[128,2,640]{2,1,0:T(2,128)(2,1)} %reshape.22), calls=%async_computation.5 | async-start | bytes 655360 | tf_op jit(solution)/shard_map/all_to_all | solution.py:222

commit v3 on v2

--- a/solution.py
+++ b/solution.py
@@ -25,34 +25,65 @@
     return lax.broadcasted_iota(jnp.int32, shape, dim)
 
 
-def route_hits(ids, node_count, slot_cap):
-    toks, routes = ids.shape
-    experts = iota((toks, node_count), 1)
-    named = jnp.zeros((toks, node_count), F32)
-    for k in range(routes):
-        named += (ids[:, k : k + 1] == experts).astype(F32)
-    before = (iota((toks, toks), 1) < iota((toks, toks), 0)).astype(BF16)
-    earlier = dot(before, named.astype(BF16))
-    slots = iota((toks, node_count * slot_cap), 1)
-    hits = []
-    for k in range(routes):
-        expert = ids[:, k : k + 1]
-        slot = jnp.sum(jnp.where(expert == experts, earlier, 0.0), axis=1, keepdims=True)
-        hits.append(slots == expert * slot_cap + slot.astype(jnp.int32))
-    return hits
-
-
-def dispatch_kernel(node_count, slot_cap, ids_ref, x_ref, y_ref, out_ref):
-    toks = ids_ref.shape[0]
-    hits = route_hits(ids_ref[...], node_count, slot_cap)
-    taken = functools.reduce(jnp.logical_or, hits).astype(F32)
+def split_three(value):
+    high = value.astype(BF16)
+    rest = value - high.astype(F32)
+    middle = rest.astype(BF16)
+    return high, middle, (rest - middle.astype(F32)).astype(BF16)
+
+
+def pack_kernel(size, ids_in, route_in, x_in, y_in, out_ref, ids_ref, route_ref, x_ref, y_ref, sems):
+    pairs = ((ids_in, ids_ref), (route_in, route_ref), (x_in, x_ref), (y_in, y_ref))
+    copies = [pltpu.make_async_copy(*pair, sems.at[i]) for i, pair in enumerate(pairs)]
+    for copy in copies:
+        copy.start()
+    for copy in copies:
+        copy.wait()
+    groups, toks, _ = out_ref.shape
+    routes = ids_ref.shape[0]
+    width = x_ref.shape[1]
+    unit = (iota((toks, toks), 0) == iota((toks, toks), 1)).astype(BF16)
+    pieces = [piece.astype(F32) for piece in split_three(route_ref[...])]
+    fill = jnp.zeros((LANES - 4 * routes, toks), F32)
+    for group in range(groups):
+        ids = (ids_ref[...] - group * size).astype(F32)
+        facts = jnp.concatenate([ids, *pieces, fill], axis=0).astype(BF16)
+        out_ref[group, :, :width] = x_ref[...]
+        out_ref[group, :, width : 2 * width] = y_ref[...]
+        out_ref[group, :, 2 * width :] = dot(unit, facts, 1, 1).astype(BF16)
+
+
+def route_hits(facts, groups, toks, size, slot_cap, routes):
+    shape = (groups * toks, size * groups * slot_cap)
+    column = iota(shape, 1)
+    expert = column // (groups * slot_cap)
+    names = [facts[:, k : k + 1].astype(jnp.int32) == expert for k in range(routes)]
+    named = functools.reduce(jnp.logical_or, names)
+    square = (groups * toks, groups * toks)
+    one, two = iota(square, 0), iota(square, 1)
+    before = ((one // toks == two // toks) & (two < one)).astype(BF16)
+    earlier = dot(before, named.astype(BF16)).astype(jnp.int32)
+    here = (earlier == column % slot_cap) & (
+        column // slot_cap % groups == iota(shape, 0) // toks
+    )
+    return [name & here for name in names], named & here
+
+
+def rows_kernel(routes, slot_cap, tok_ref, out_ref):
+    groups, toks, full = tok_ref.shape
+    size = out_ref.shape[0]
+    width = full - LANES
+    toks_all = tok_ref[...].reshape(groups * toks, full)
+    facts = toks_all[:, width:].astype(F32)
+    _, taken = route_hits(facts, groups, toks, size, slot_cap, routes)
+    taken = taken.astype(F32)
     free = 1.0 - jnp.sum(taken, axis=0, keepdims=True)
-    free = jnp.where(iota(taken.shape, 0) == 0, jnp.broadcast_to(free, taken.shape), 0.0)
+    shape = (EXTRA, taken.shape[1])
+    free = jnp.where(iota(shape, 0) == 0, jnp.broadcast_to(free, shape), 0.0)
     pick = jnp.concatenate([taken, free], axis=0).astype(BF16)
-    width = x_ref.shape[1]
-    for place, ref in enumerate((x_ref, y_ref)):
-        rows = jnp.concatenate([ref[...], jnp.full((toks, width), EMPTY, BF16)], axis=0)
-        out_ref[:, place * width : (place + 1) * width] = dot(pick, rows, 0, 0).astype(BF16)
+    rows = jnp.concatenate([toks_all[:, :width], jnp.full((EXTRA, width), EMPTY, BF16)], axis=0)
+    picked = dot(pick, rows, 0, 0).astype(BF16)
+    out_ref[...] = picked.reshape(out_ref.shape)
 
 
 def parts_kernel(rows_ref, gate_ref, up_ref, down_ref, main_ref, rest_ref, place_ref, count_ref):
@@ -143,27 +174,36 @@
     out_ref[:, width:] = dot(place_ref[...], score).astype(BF16)
 
 
-def home_kernel(node_count, slot_cap, ids_ref, route_ref, back_ref, grad_ref, score_ref):
-    width = grad_ref.shape[1]
-    toks, routes = ids_ref.shape
-    hits = route_hits(ids_ref[...], node_count, slot_cap)
+def combine_kernel(routes, slot_cap, tok_ref, back_ref, out_ref):
+    groups, toks, full = tok_ref.shape
+    size = back_ref.shape[0]
+    width = back_ref.shape[2] - LANES
+    facts = tok_ref[:, :, full - LANES :].reshape(groups * toks, LANES).astype(F32)
+    back = back_ref[...].reshape(size * groups * slot_cap, width + LANES)
+    hits, _ = route_hits(facts, groups, toks, size, slot_cap, routes)
     weight = jnp.zeros(hits[0].shape, F32)
     for k in range(routes):
-        weight += jnp.where(hits[k], route_ref[:, k : k + 1], 0.0)
-    high = weight.astype(BF16)
-    rest = weight - high.astype(F32)
-    middle = rest.astype(BF16)
-    low = (rest - middle.astype(F32)).astype(BF16)
-    split = jnp.concatenate([high, middle, low], axis=0)
-    sums = dot(split, back_ref[:, :width])
-    grad_ref[...] = (sums[:toks] + sums[toks : 2 * toks] + sums[2 * toks :]).astype(BF16)
-    picks = jnp.concatenate([hit.astype(BF16) for hit in hits], axis=0)
-    scores = dot(picks, back_ref[:, width:])
-    lane = iota((toks, LANES), 1)
-    placed = jnp.zeros((toks, LANES), F32)
+        value = sum(facts[:, i * routes + k : i * routes + k + 1] for i in (1, 2, 3))
+        weight = jnp.where(hits[k], value, weight)
+    sums = sum(dot(piece, back[:, :width]) for piece in split_three(weight))
+    lane = iota((groups * toks, LANES), 1)
+    scores = jnp.zeros((groups * toks, LANES), F32)
     for k in range(routes):
-        placed = jnp.where(lane == k, scores[k * toks : (k + 1) * toks], placed)
-    score_ref[...] = placed[:, :routes].astype(BF16)
+        scores = jnp.where(lane == k, dot(hits[k].astype(BF16), back[:, width:]), scores)
+    out_ref[:, :, :width] = sums.astype(BF16).reshape(groups, toks, width)
+    out_ref[:, :, width:] = scores.astype(BF16).reshape(groups, toks, LANES)
+
+
+def home_kernel(parts_ref, grad_ref, score_ref):
+    groups, toks, _ = parts_ref.shape
+    width = grad_ref.shape[1]
+    total = parts_ref[0].astype(F32)
+    for group in range(1, groups):
+        total += parts_ref[group].astype(F32)
+    grad_ref[...] = total[:, :width].astype(BF16)
+    unit = (iota((toks, toks), 0) == iota((toks, toks), 1)).astype(BF16)
+    scores = dot(total[:, width:].astype(BF16), unit, 0, 0)
+    score_ref[...] = scores[: score_ref.shape[0]].astype(BF16)
 
 
 def on_device(hidden_in, grad_out, expert_ids, route_weights, gate_weight, up_weight, down_weight):
@@ -171,8 +211,18 @@
     parts = lax.axis_size("local")
     tok_count, width = hidden_in.shape
     group_count = min(8, node_count // 2)
-    slot_cap = 2 * tok_count // (node_count // group_count)
+    group_size = node_count // group_count
+    slot_cap = 2 * tok_count // group_size
     slot_total = node_count * slot_cap
+    routes = expert_ids.shape[1]
+    across = [[g * group_size + p for g in range(group_count)] for p in range(group_size)]
+    within = [[g * group_size + p for p in range(group_size)] for g in range(group_count)]
+
+    def swap(value, axis, members=None):
+        return lax.all_to_all(
+            value, axis, split_axis=0, concat_axis=0, tiled=True, axis_index_groups=members
+        )
+
     w_gate, w_up, w_down = gate_weight[0], up_weight[0], down_weight[0]
 
     def call(kernel, shape, *args):
@@ -182,12 +232,21 @@
             compiler_params=PARAMS,
         )(*args)
 
-    send = call(
-        functools.partial(dispatch_kernel, node_count, slot_cap),
-        (slot_total, 2 * width), expert_ids, hidden_in, grad_out,
-    ).reshape(node_count, slot_cap, 2 * width)
-    recv = lax.all_to_all(send, "node", split_axis=0, concat_axis=0, tiled=True)
-    rows = recv.reshape(slot_total, 2 * width)
+    own = (expert_ids.T, route_weights.T, hidden_in, grad_out)
+    tokens = pl.pallas_call(
+        functools.partial(pack_kernel, group_size),
+        out_shape=jax.ShapeDtypeStruct((group_count, tok_count, 2 * width + LANES), BF16),
+        in_specs=[pl.BlockSpec(memory_space=pltpu.HBM)] * len(own),
+        scratch_shapes=[pltpu.VMEM(value.shape, value.dtype) for value in own]
+        + [pltpu.SemaphoreType.DMA((len(own),))],
+        compiler_params=pltpu.CompilerParams(vmem_limit_bytes=56 * 1024 * 1024),
+    )(*own)
+    tokens = swap(tokens, "node", across)
+    rows = call(
+        functools.partial(rows_kernel, routes, slot_cap),
+        (group_size, group_count * slot_cap, 2 * width), tokens,
+    )
+    rows = swap(rows, "node", within).reshape(slot_total, 2 * width)
     main = max(EXTRA, slot_total * 5 // 8 // EXTRA * EXTRA)
     vmem = pl.BlockSpec(memory_space=pltpu.VMEM)
     main_sums, rest_sums, place, count = pl.pallas_call(
@@ -203,9 +262,9 @@
     )(rows, w_gate, w_up, w_down)
 
     def over_local(sums):
-        sums = lax.all_to_all(sums, "local", split_axis=0, concat_axis=0, tiled=True)
+        sums = swap(sums, "local")
         hidden = call(hidden_kernel, (parts, sums.shape[1] + EXTRA, 2 * LANES), sums)
-        return lax.all_to_all(hidden, "local", split_axis=0, concat_axis=0, tiled=True)
+        return swap(hidden, "local")
 
     def rest_of(sums, w_gate, w_up):
         return call(rest_kernel, (slot_total - main, width + LANES), over_local(sums), w_gate, w_up)
@@ -218,14 +277,14 @@
     )
     hidden = over_local(main_sums)
     back = call(back_kernel, (slot_total, width + LANES), hidden, w_gate, w_up, rest, place)
-    back = back.reshape(node_count, slot_cap, width + LANES)
-    home = lax.all_to_all(back, "node", split_axis=0, concat_axis=0, tiled=True)
-    home = home.reshape(slot_total, width + LANES)
-    grad_in, grad_weights = call(
-        functools.partial(home_kernel, node_count, slot_cap),
-        [(tok_count, width), (tok_count, expert_ids.shape[1])], expert_ids, route_weights, home,
-    )
-    return (grad_in, grad_weights)
+    back = swap(back.reshape(group_size, group_count * slot_cap, width + LANES), "node", within)
+    home = call(
+        functools.partial(combine_kernel, routes, slot_cap),
+        (group_count, tok_count, width + LANES), tokens, back,
+    )
+    home = swap(home, "node", across)
+    grad_in, scores = call(home_kernel, [(tok_count, width), (routes, tok_count)], home)
+    return (grad_in, scores.T)
 
 
 def solution(mesh):

time: 161 us -> 159 us (0.988)
  the two profiles are of different devices: /device:TPU:7 before, /device:TPU:8 now
where the time goes in v3:
time: 159 us; the launch traced here: 158 us
  blocking collectives  131 us (82%)
  waiting for transfers between devices  10.9 us (7%)
  Pallas kernels  10.3 us (6%)
  starting transfers between devices  4.4 us (3%)
    all_to_all x5, blocking collectives, swap(): lax.all_to_all(value, axis, split_axis=0, concat_axis=0, tiled=True, axis...  131 us
    all_to_all x1, waiting for transfers between devices, swap(): lax.all_to_all(value, axis, split_axis=0, concat_axis=0, tiled=True, axis...  10.9 us
    pallas_call x5, Pallas kernels, call(): pl.pallas_call(kernel, out_shape=jax.tree.map(lambda s: jax.ShapeDtypeStr...  4.84 us
    all_to_all x1, starting transfers between devices, swap(): lax.all_to_all(value, axis, split_axis=0, concat_axis=0, tiled=True, axis...  4.4 us
    pallas_call x1, Pallas kernels, on_device(): pl.pallas_call(parts_kernel, out_shape=[jax.ShapeDtypeStruct((parts, main...  3.82 us
  transfers between devices with their start and end apart: 1, of which 1 were waited for; matrix products, arithmetic and copies ran while one was open for 0% of the time, Pallas kernels for 0%

profile of v3, /device:TPU:8, one launch (start us, length us, event | category | flops | bytes accessed | tf_op | source)
XLA Modules:
  0.0 158.2 jit_solution(2978241665596308810)
XLA Ops:
  0.6 1.7 %shard_map.86 = bf16[8,16,1152]{2,1,0:T(8,128)(2,1)} custom-call(s32[8,16]{1,0:T(8,128)} %bitcast.18, f32[8,16]{1,0:T(8,128)} %bitcast.19, bf16[16,512]{1,0:T(8,128)(2,1)} %x_in.1, bf16[16,512]{1,0:T(8,128)(2,1)} %y_in.1), custom_call_target="tpu_custom_call" | custom-call | tf_op jit(solution)/shard_map/pallas_call | solution.py:236
  2.3 42.4 %all_to_all.40.tok_ref = bf16[8,16,1152]{2,1,0:T(8,128)(2,1)S(1)} all-to-all(bf16[8,16,1152]{2,1,0:T(8,128)(2,1)} %shard_map.86), channel_id=1, replica_groups={{0,128,256,384,512,640,768,896},{8,136,264,392,520,648,776,904},{16,144..., dimensions={0} | all-to-all | bytes 589824 | tf_op jit(solution)/shard_map/all_to_all | solution.py:222
  44.7 0.0 copy-start
  44.7 1.6 shard_map.87
  46.3 4.4 %all-to-all-start.3 = ((bf16[16,16,1024]{2,1,0:T(8,128)(2,1)}), bf16[16,16,1024]{2,1,0:T(8,128)(2,1)S(1)}, u32[]{:S(2)}, u32[]{:S(2)}) async-start(bf16[16,16,1024]{2,1,0:T(8,128)(2,1)} %shard_map.87), calls=%async_computation.3 | async-start | bytes 1048576 | tf_op jit(solution)/shard_map/all_to_all | solution.py:222
  50.7 10.9 %all-to-all-done.3 = bf16[16,16,1024]{2,1,0:T(8,128)(2,1)S(1)} async-done(((bf16[16,16,1024]{2,1,0:T(8,128)(2,1)}), bf16[16,16,1024]{2,1,0:T(8,128)(2,1)S(1)}, u32[]{:S(2)}, u32[]{:S(2)}) %all-to-all-start.3) | async-done | bytes 524320 | tf_op jit(solution)/shard_map/all_to_all | solution.py:222
  61.6 0.0 copy-done
  61.6 3.8 %shard_map.88 = (bf16[8,160,384]{2,1,0:T(8,128)(2,1)S(1)}, bf16[8,96,384]{2,1,0:T(8,128)(2,1)}, bf16[256,256]{1,0:T(8,128)(2,1)S(1)}, s32[1,1]{1,0:T(1,128)}) custom-call(bf16[256,1024]{1,0:T(8,128)(2,1)S(1)} %bitcast.9, bf16[512,1024]{1,0:T(8,128)(2,1)} %bitcast.12, bf16[512,1024]{1,0:T(8,128)(2,1)} %bitcast.15, bf16[1024,512]{1,0:T(8,128)(2,1)S(1)} %bitcast.11), custom_call_target="tpu_custom_call" | custom-call | tf_op jit(solution)/shard_map/pallas_call | solution.py:252
  66.1 32.7 %all_to_all.41.parts_ref = bf16[8,160,384]{2,1,0:T(8,128)(2,1)S(1)} all-to-all(bf16[8,160,384]{2,1,0:T(8,128)(2,1)S(1)} %get-tuple-element.20), channel_id=1, replica_groups=mesh['node'=128,'local'=8] {'local'}, dimensions={0} | all-to-all | bytes 1966080 | tf_op jit(solution)/shard_map/all_to_all | solution.py:222
  98.8 0.0 copy-start.3
  98.8 0.4 shard_map.89
  99.2 0.0 copy-start.1
  99.2 22.6 %all_to_all.42.hidden_ref = bf16[8,176,256]{2,1,0:T(8,128)(2,1)S(1)} all-to-all(bf16[8,176,256]{2,1,0:T(8,128)(2,1)S(1)} %shard_map.89), channel_id=1, replica_groups=mesh['node'=128,'local'=8] {'local'}, dimensions={0} | all-to-all | bytes 1441792 | tf_op jit(solution)/shard_map/all_to_all | solution.py:222
  121.8 0.0 copy-done.3
  121.9 0.0 copy-done.1
  121.9 1.1 shard_map.90
  123.0 13.8 %all_to_all.43.back_ref = bf16[16,16,640]{2,1,0:T(8,128)(2,1)S(1)} all-to-all(bf16[16,16,640]{2,1,0:T(8,128)(2,1)S(1)} %bitcast.10), channel_id=1, replica_groups={{0,8,16,24,32,40,48,56,64,72,80,88,96,104,112,120},{128,136,144,152,160..., dimensions={0} | all-to-all | bytes 655360 | tf_op jit(solution)/shard_map/all_to_all | solution.py:222
  136.8 1.0 shard_map.91
  137.8 19.7 %all_to_all.44.parts_ref = bf16[8,16,640]{2,1,0:T(8,128)(2,1)S(1)} all-to-all(bf16[8,16,640]{2,1,0:T(8,128)(2,1)S(1)} %shard_map.91), channel_id=1, replica_groups={{0,128,256,384,512,640,768,896},{8,136,264,392,520,648,776,904},{16,144..., dimensions={0} | all-to-all | bytes 327680 | tf_op jit(solution)/shard_map/all_to_all | solution.py:222
  157.4 0.8 shard_map.92
  (2 shorter events, 0.0 us)
Async XLA Ops:
  44.7 16.9 %copy-start = (bf16[1,1024,512]{2,1,0:T(8,128)(2,1)S(1)}, bf16[1,1024,512]{2,1,0:T(8,128)(2,1)}, u32[]{:S(2)}) copy-start(bf16[1,1024,512]{2,1,0:T(8,128)(2,1)} %param.15) | copy-start | bytes 3145732
  46.3 15.3 %all-to-all-start.3 = ((bf16[16,16,1024]{2,1,0:T(8,128)(2,1)}), bf16[16,16,1024]{2,1,0:T(8,128)(2,1)S(1)}, u32[]{:S(2)}, u32[]{:S(2)}) async-start(bf16[16,16,1024]{2,1,0:T(8,128)(2,1)} %shard_map.87), calls=%async_computation.3 | async-start | bytes 1048576 | tf_op jit(solution)/shard_map/all_to_all | solution.py:222
  98.8 23.0 %copy-start.3 = (bf16[1,512,1024]{2,1,0:T(8,128)(2,1)S(1)}, bf16[1,512,1024]{2,1,0:T(8,128)(2,1)}, u32[]{:S(2)}) copy-start(bf16[1,512,1024]{2,1,0:T(8,128)(2,1)} %param.14) | copy-start | bytes 3145732
  99.2 22.7 %copy-start.1 = (bf16[1,512,1024]{2,1,0:T(8,128)(2,1)S(1)}, bf16[1,512,1024]{2,1,0:T(8,128)(2,1)}, u32[]{:S(2)}) copy-start(bf16[1,512,1024]{2,1,0:T(8,128)(2,1)} %param.13) | copy-start | bytes 3145732

commit v4 on v3

--- a/solution.py
+++ b/solution.py
@@ -86,32 +86,53 @@
     out_ref[...] = picked.reshape(out_ref.shape)
 
 
-def parts_kernel(rows_ref, gate_ref, up_ref, down_ref, main_ref, rest_ref, place_ref, count_ref):
-    parts, main, _ = main_ref.shape
+def products(x, y, gate_ref, up_ref, down_ref, out_ref):
+    parts = out_ref.shape[0]
+    for j in range(0, parts, 2):
+        step = min(2, parts - j)
+        cols = slice(j * LANES, (j + step) * LANES)
+        values = (
+            dot(x, gate_ref[:, cols]),
+            dot(y, down_ref[cols, :], 1, 1),
+            dot(x, up_ref[:, cols]),
+        )
+        for i in range(step):
+            for at, value in zip((0, 2, 1), values):
+                out_ref[j + i, :, at * LANES : (at + 1) * LANES] = value[
+                    :, i * LANES : (i + 1) * LANES
+                ].astype(BF16)
+
+
+def parts_kernel(
+    rows_ref, gate_ref, up_in, down_ref, main_ref, rest_out, place_ref, count_ref, up_ref, rest_ref, sems
+):
+    up_copy = pltpu.make_async_copy(up_in, up_ref, sems.at[0])
+    up_copy.start()
+    main = main_ref.shape[1]
     slots = rows_ref.shape[0]
     width = gate_ref.shape[0]
     named = rows_ref[:, :LANES].astype(F32)[:, :1] < 0.5 * EMPTY
     named_wide = jnp.broadcast_to(named.astype(F32), (slots, LANES))
+    count = jnp.sum(named_wide[:, :1]).astype(jnp.int32)
+    count_ref[0, 0] = count
     before = (iota((slots, slots), 1) < iota((slots, slots), 0)).astype(BF16)
     order = dot(before, named_wide.astype(BF16))[:, :1].astype(jnp.int32)
     place = (jnp.where(named, order, slots) == iota((slots, slots), 1)).astype(BF16)
     place_ref[...] = place
-    count_ref[0, 0] = jnp.sum(named_wide[:, :1]).astype(jnp.int32)
-    x = dot(place, rows_ref[:, :width], 0, 0).astype(BF16)
-    y = dot(place, rows_ref[:, width:], 0, 0).astype(BF16)
-    for j in range(0, parts, 2):
-        step = min(2, parts - j)
-        cols = slice(j * LANES, (j + step) * LANES)
-        products = (
-            dot(x, gate_ref[:, cols]),
-            dot(x, up_ref[:, cols]),
-            dot(y, down_ref[cols, :], 1, 1),
-        )
-        for i in range(step):
-            for at, value in enumerate(products):
-                piece = value[:, i * LANES : (i + 1) * LANES].astype(BF16)
-                main_ref[j + i, :, at * LANES : (at + 1) * LANES] = piece[:main]
-                rest_ref[j + i, :, at * LANES : (at + 1) * LANES] = piece[main:]
+    x = dot(place[:, :main], rows_ref[:, :width], 0, 0).astype(BF16)
+    y = dot(place[:, :main], rows_ref[:, width:], 0, 0).astype(BF16)
+    up_copy.wait()
+    products(x, y, gate_ref, up_ref, down_ref, main_ref)
+
+    @pl.when(count > main)
+    def _():
+        last = place_ref[:, main:]
+        x = dot(last, rows_ref[:, :width], 0, 0).astype(BF16)
+        y = dot(last, rows_ref[:, width:], 0, 0).astype(BF16)
+        products(x, y, gate_ref, up_ref, down_ref, rest_ref)
+        rest_copy = pltpu.make_async_copy(rest_ref, rest_out, sems.at[1])
+        rest_copy.start()
+        rest_copy.wait()
 
 
 def hidden_kernel(parts_ref, out_ref):
@@ -160,18 +181,21 @@
     return total.astype(BF16), dot(unit, spread, 1, 1).astype(BF16)
 
 
-def rest_kernel(hidden_ref, gate_ref, up_ref, out_ref):
+def back_kernel(hidden_ref, gate_ref, up_ref, place_ref, count_ref, out_ref, count_out):
+    count_out[0, 0] = count_ref[0, 0]
     width = gate_ref.shape[0]
-    out_ref[:, :width], out_ref[:, width:] = back_rows(hidden_ref, gate_ref, up_ref)
-
-
-def back_kernel(hidden_ref, gate_ref, up_ref, rest_ref, place_ref, out_ref):
+    rows, score = back_rows(hidden_ref, gate_ref, up_ref)
+    place = place_ref[:, : rows.shape[0]]
+    out_ref[:, :width] = dot(place, rows).astype(BF16)
+    out_ref[:, width:] = dot(place, score).astype(BF16)
+
+
+def rest_kernel(hidden_ref, gate_ref, up_ref, place_ref, main_ref, out_ref):
     width = gate_ref.shape[0]
-    main, main_score = back_rows(hidden_ref, gate_ref, up_ref)
-    rows = jnp.concatenate([main, rest_ref[:, :width]], axis=0)
-    out_ref[:, :width] = dot(place_ref[...], rows).astype(BF16)
-    score = jnp.concatenate([main_score, rest_ref[:, width:]], axis=0)
-    out_ref[:, width:] = dot(place_ref[...], score).astype(BF16)
+    rows, score = back_rows(hidden_ref, gate_ref, up_ref)
+    place = place_ref[:, place_ref.shape[1] - rows.shape[0] :]
+    out_ref[:, :width] = (main_ref[:, :width].astype(F32) + dot(place, rows)).astype(BF16)
+    out_ref[:, width:] = (main_ref[:, width:].astype(F32) + dot(place, score)).astype(BF16)
 
 
 def combine_kernel(routes, slot_cap, tok_ref, back_ref, out_ref):
@@ -218,6 +242,10 @@
     across = [[g * group_size + p for g in range(group_count)] for p in range(group_size)]
     within = [[g * group_size + p for p in range(group_size)] for g in range(group_count)]
 
+    vmem = pl.BlockSpec(memory_space=pltpu.VMEM)
+    smem = pl.BlockSpec(memory_space=pltpu.SMEM)
+    hbm = pl.BlockSpec(memory_space=pltpu.HBM)
+
     def swap(value, axis, members=None):
         return lax.all_to_all(
             value, axis, split_axis=0, concat_axis=0, tiled=True, axis_index_groups=members
@@ -236,7 +264,7 @@
     tokens = pl.pallas_call(
         functools.partial(pack_kernel, group_size),
         out_shape=jax.ShapeDtypeStruct((group_count, tok_count, 2 * width + LANES), BF16),
-        in_specs=[pl.BlockSpec(memory_space=pltpu.HBM)] * len(own),
+        in_specs=[hbm] * len(own),
         scratch_shapes=[pltpu.VMEM(value.shape, value.dtype) for value in own]
         + [pltpu.SemaphoreType.DMA((len(own),))],
         compiler_params=pltpu.CompilerParams(vmem_limit_bytes=56 * 1024 * 1024),
@@ -248,16 +276,22 @@
     )
     rows = swap(rows, "node", within).reshape(slot_total, 2 * width)
     main = max(EXTRA, slot_total * 5 // 8 // EXTRA * EXTRA)
-    vmem = pl.BlockSpec(memory_space=pltpu.VMEM)
+    rest_shape = (parts, slot_total - main, 3 * LANES)
     main_sums, rest_sums, place, count = pl.pallas_call(
         parts_kernel,
         out_shape=[
             jax.ShapeDtypeStruct((parts, main, 3 * LANES), BF16),
-            jax.ShapeDtypeStruct((parts, slot_total - main, 3 * LANES), BF16),
+            jax.ShapeDtypeStruct(rest_shape, BF16),
             jax.ShapeDtypeStruct((slot_total, slot_total), BF16),
             jax.ShapeDtypeStruct((1, 1), jnp.int32),
         ],
-        out_specs=[vmem, vmem, vmem, pl.BlockSpec(memory_space=pltpu.SMEM)],
+        in_specs=[vmem, vmem, hbm, vmem],
+        out_specs=[vmem, hbm, vmem, smem],
+        scratch_shapes=[
+            pltpu.VMEM(w_up.shape, BF16),
+            pltpu.VMEM(rest_shape, BF16),
+            pltpu.SemaphoreType.DMA((2,)),
+        ],
         compiler_params=PARAMS,
     )(rows, w_gate, w_up, w_down)
 
@@ -266,17 +300,24 @@
         hidden = call(hidden_kernel, (parts, sums.shape[1] + EXTRA, 2 * LANES), sums)
         return swap(hidden, "local")
 
-    def rest_of(sums, w_gate, w_up):
-        return call(rest_kernel, (slot_total - main, width + LANES), over_local(sums), w_gate, w_up)
-
-    rest = lax.cond(
-        count[0, 0] > main,
-        rest_of,
-        lambda *_: jnp.zeros((slot_total - main, width + LANES), BF16),
-        rest_sums, w_gate, w_up,
-    )
     hidden = over_local(main_sums)
-    back = call(back_kernel, (slot_total, width + LANES), hidden, w_gate, w_up, rest, place)
+    back, count = pl.pallas_call(
+        back_kernel,
+        out_shape=[
+            jax.ShapeDtypeStruct((slot_total, width + LANES), BF16),
+            jax.ShapeDtypeStruct((1, 1), jnp.int32),
+        ],
+        in_specs=[vmem, vmem, vmem, vmem, smem],
+        out_specs=[vmem, smem],
+        compiler_params=PARAMS,
+    )(hidden, w_gate, w_up, place, count)
+
+    def add_rest(back, sums, place, w_gate, w_up):
+        return call(rest_kernel, (slot_total, width + LANES), over_local(sums), w_gate, w_up, place, back)
+
+    back = lax.cond(
+        count[0, 0] > main, add_rest, lambda back, *_: back, back, rest_sums, place, w_gate, w_up
+    )
     back = swap(back.reshape(group_size, group_count * slot_cap, width + LANES), "node", within)
     home = call(
         functools.partial(combine_kernel, routes, slot_cap),

time: 159 us -> 157 us (0.987)
  blocking collectives: 131 us -> 146 us
  waiting for transfers between devices: 10.9 us -> 0 us
  starting transfers between devices: 4.4 us -> 0 us
    all_to_all x5 -> x6, blocking collectives: 131 us -> 146 us  [swap(): lax.all_to_all(value, axis, split_axis=0, concat_axis=0, tiled=True, axis...]
    all_to_all x1 -> x0, waiting for transfers between devices: 10.9 us -> none  [swap(): lax.all_to_all(value, axis, split_axis=0, concat_axis=0, tiled=True, axis...]
    all_to_all x1 -> x0, starting transfers between devices: 4.4 us -> none  [swap(): lax.all_to_all(value, axis, split_axis=0, concat_axis=0, tiled=True, axis...]
    pallas_call x5 -> x4, Pallas kernels: 4.84 us -> 2.92 us  [call(): pl.pallas_call(kernel, out_shape=jax.tree.map(lambda s: jax.ShapeDtypeStr...]
    pallas_call x0 -> x1, Pallas kernels: none -> 1.76 us  [on_device(): pl.pallas_call(back_kernel, out_shape=[jax.ShapeDtypeStruct((slot_total,...]
  transfers between devices with their start and end apart: 1 -> 0, of which waited for: 1 -> 0; matrix products, arithmetic and copies ran while one was open for 0% -> 0% of each run, Pallas kernels for 0% -> 0%
where the time goes in v4:
time: 157 us
  blocking collectives  146 us (93%)
  Pallas kernels  8.95 us (6%)
    all_to_all x6, blocking collectives, swap(): lax.all_to_all(value, axis, split_axis=0, concat_axis=0, tiled=True, axis...  146 us

profile of v4, /device:TPU:8, one launch (start us, length us, event | category | flops | bytes accessed | tf_op | source)
XLA Modules:
  0.0 156.8 jit_solution(5596082701389789146)
XLA Ops:
  0.6 1.7 %shard_map.86 = bf16[8,16,1152]{2,1,0:T(8,128)(2,1)} custom-call(s32[8,16]{1,0:T(8,128)} %bitcast.18, f32[8,16]{1,0:T(8,128)} %bitcast.19, bf16[16,512]{1,0:T(8,128)(2,1)} %x_in.1, bf16[16,512]{1,0:T(8,128)(2,1)} %y_in.1), custom_call_target="tpu_custom_call" | custom-call | tf_op jit(solution)/shard_map/pallas_call | solution.py:264
  2.3 0.0 copy-start.1
  2.3 42.5 %all_to_all.39.tok_ref = bf16[8,16,1152]{2,1,0:T(8,128)(2,1)S(1)} all-to-all(bf16[8,16,1152]{2,1,0:T(8,128)(2,1)} %shard_map.86), channel_id=1, replica_groups={{0,128,256,384,512,640,768,896},{8,136,264,392,520,648,776,904},{16,144..., dimensions={0} | all-to-all | bytes 589824 | tf_op jit(solution)/shard_map/all_to_all | solution.py:250
  44.9 0.0 copy-start
  44.9 0.8 shard_map.87
  45.6 15.1 %all_to_all.40 = bf16[16,16,1024]{2,1,0:T(8,128)(2,1)S(1)} all-to-all(bf16[16,16,1024]{2,1,0:T(8,128)(2,1)S(1)} %shard_map.87), channel_id=1, replica_groups={{0,8,16,24,32,40,48,56,64,72,80,88,96,104,112,120},{128,136,144,152,160..., dimensions={0} | all-to-all | bytes 1048576 | tf_op jit(solution)/shard_map/all_to_all | solution.py:250
  60.7 0.0 copy-done.1
  60.7 0.0 copy-done
  60.7 2.6 %shard_map.88 = (bf16[8,160,384]{2,1,0:T(8,128)(2,1)S(1)}, bf16[8,96,384]{2,1,0:T(8,128)(2,1)S(1)}, bf16[256,256]{1,0:T(8,128)(2,1)S(1)}, s32[1,1]{1,0:T(1,128)}) custom-call(bf16[256,1024]{1,0:T(8,128)(2,1)S(1)} %bitcast.9, bf16[512,1024]{1,0:T(8,128)(2,1)S(1)} %bitcast.11, bf16[512,1024]{1,0:T(8,128)(2,1)} %bitcast.14, bf16[1024,512]{1,0:T(8,128)(2,1)S(1)} %bitcast.10), custom_call_target="tpu_custom_call" | custom-call | tf_op jit(solution)/shard_map/pallas_call | solution.py:280
  63.3 32.7 %all_to_all.41.parts_ref = bf16[8,160,384]{2,1,0:T(8,128)(2,1)S(1)} all-to-all(bf16[8,160,384]{2,1,0:T(8,128)(2,1)S(1)} %get-tuple-element.29), channel_id=1, replica_groups=mesh['node'=128,'local'=8] {'local'}, dimensions={0} | all-to-all | bytes 1966080 | tf_op jit(solution)/shard_map/all_to_all | solution.py:250
  96.0 0.4 shard_map.89
  96.4 0.0 copy-start.2
  96.4 22.6 %all_to_all.42.hidden_ref = bf16[8,176,256]{2,1,0:T(8,128)(2,1)S(1)} all-to-all(bf16[8,176,256]{2,1,0:T(8,128)(2,1)S(1)} %shard_map.89), channel_id=1, replica_groups=mesh['node'=128,'local'=8] {'local'}, dimensions={0} | all-to-all | bytes 1441792 | tf_op jit(solution)/shard_map/all_to_all | solution.py:250
  119.1 0.0 copy-done.2
  119.1 1.8 %shard_map.90 = (bf16[256,640]{1,0:T(8,128)(2,1)S(1)}, s32[1,1]{1,0:T(1,128)}) custom-call(bf16[8,176,256]{2,1,0:T(8,128)(2,1)S(1)} %all_to_all.42.hidden_ref, bf16[512,1024]{1,0:T(8,128)(2,1)S(1)} %bitcast.12, bf16[512,1024]{1,0:T(8,128)(2,1)S(1)} %bitcast.15, bf16[256,256]{1,0:T(8,128)(2,1)S(1)} %get-tuple-element.30.place_ref, ...), custom_call_target="tpu_custom_call" | custom-call | tf_op jit(solution)/shard_map/pallas_call | solution.py:304
  121.5 13.8 %all_to_all.43.back_ref = bf16[16,16,640]{2,1,0:T(8,128)(2,1)S(1)} all-to-all(bf16[16,16,640]{2,1,0:T(8,128)(2,1)S(1)} %bitcast.17), channel_id=1, replica_groups={{0,8,16,24,32,40,48,56,64,72,80,88,96,104,112,120},{128,136,144,152,160..., dimensions={0} | all-to-all | bytes 655360 | tf_op jit(solution)/shard_map/all_to_all | solution.py:250
  135.3 1.0 shard_map.91
  136.3 19.7 %all_to_all.44.parts_ref = bf16[8,16,640]{2,1,0:T(8,128)(2,1)S(1)} all-to-all(bf16[8,16,640]{2,1,0:T(8,128)(2,1)S(1)} %shard_map.91), channel_id=1, replica_groups={{0,128,256,384,512,640,768,896},{8,136,264,392,520,648,776,904},{16,144..., dimensions={0} | all-to-all | bytes 327680 | tf_op jit(solution)/shard_map/all_to_all | solution.py:250
  156.0 0.8 shard_map.92
  (1 shorter events, 0.0 us)
Async XLA Ops:
  2.3 58.4 %copy-start.1 = (bf16[1,512,1024]{2,1,0:T(8,128)(2,1)S(1)}, bf16[1,512,1024]{2,1,0:T(8,128)(2,1)}, u32[]{:S(2)}) copy-start(bf16[1,512,1024]{2,1,0:T(8,128)(2,1)} %param.13) | copy-start | bytes 3145732
  44.9 15.9 %copy-start = (bf16[1,1024,512]{2,1,0:T(8,128)(2,1)S(1)}, bf16[1,1024,512]{2,1,0:T(8,128)(2,1)}, u32[]{:S(2)}) copy-start(bf16[1,1024,512]{2,1,0:T(8,128)(2,1)} %param.15) | copy-start | bytes 3145732
  96.4 22.7 %copy-start.2 = (bf16[1,512,1024]{2,1,0:T(8,128)(2,1)S(1)}, bf16[1,512,1024]{2,1,0:T(8,128)(2,1)}, u32[]{:S(2)}) copy-start(bf16[1,512,1024]{2,1,0:T(8,128)(2,1)} %param.14) | copy-start | bytes 3145732

commit v5 on v4

--- a/solution.py
+++ b/solution.py
@@ -12,6 +12,7 @@
 EMPTY = 64.0
 LANES = 128
 EXTRA = 16
+TAIL = 8
 PARAMS = pltpu.CompilerParams(vmem_limit_bytes=32 * 1024 * 1024)
 
 
@@ -119,16 +120,15 @@
     order = dot(before, named_wide.astype(BF16))[:, :1].astype(jnp.int32)
     place = (jnp.where(named, order, slots) == iota((slots, slots), 1)).astype(BF16)
     place_ref[...] = place
-    x = dot(place[:, :main], rows_ref[:, :width], 0, 0).astype(BF16)
-    y = dot(place[:, :main], rows_ref[:, width:], 0, 0).astype(BF16)
+    packed = dot(place, rows_ref[...], 0, 0).astype(BF16)
+    x, y = packed[:main, :width], packed[:main, width:]
     up_copy.wait()
     products(x, y, gate_ref, up_ref, down_ref, main_ref)
 
     @pl.when(count > main)
     def _():
-        last = place_ref[:, main:]
-        x = dot(last, rows_ref[:, :width], 0, 0).astype(BF16)
-        y = dot(last, rows_ref[:, width:], 0, 0).astype(BF16)
+        packed = dot(place_ref[...], rows_ref[...], 0, 0).astype(BF16)
+        x, y = packed[main:, :width], packed[main:, width:]
         products(x, y, gate_ref, up_ref, down_ref, rest_ref)
         rest_copy = pltpu.make_async_copy(rest_ref, rest_out, sems.at[1])
         rest_copy.start()
@@ -153,8 +153,8 @@
         preferred_element_type=F32, precision=lax.Precision.HIGHEST,
     )
     high = score.astype(BF16).astype(F32)
-    tail = jnp.concatenate([high, score - high], axis=0).astype(BF16)
-    pad = jnp.zeros((EXTRA, 2 * LANES - rows), BF16) if rows < 2 * LANES else None
+    tail = jnp.where(iota(score.shape, 0) < 4, high, score - high).astype(BF16)
+    pad = jnp.zeros((TAIL, 2 * LANES - rows), BF16) if rows < 2 * LANES else None
     if pad is not None:
         tail = jnp.concatenate([tail, pad], axis=1)
     for j in range(parts):
@@ -165,17 +165,16 @@
 
 def back_rows(hidden_ref, gate_ref, up_ref):
     parts, rows, _ = hidden_ref.shape
-    rows -= EXTRA
+    rows -= TAIL
     width = gate_ref.shape[0]
     total = jnp.zeros((rows, width), F32)
-    score = jnp.zeros((8, 2 * LANES), F32)
+    tails = jnp.zeros((TAIL, 2 * LANES), F32)
     for j in range(parts):
         cols = slice(j * LANES, (j + 1) * LANES)
         weights = jnp.concatenate([gate_ref[:, cols], up_ref[:, cols]], axis=1)
         total += dot(hidden_ref[j, :rows, :], weights, 1, 1)
-        tail = hidden_ref[j, rows:, :].astype(F32)
-        score += tail[:8] + tail[8:]
-    score = score.astype(BF16)
+        tails += hidden_ref[j, rows:, :].astype(F32)
+    score = jnp.broadcast_to(tails[:1] + tails[4:5], tails.shape).astype(BF16)
     unit = (iota((rows, 2 * LANES), 0) == iota((rows, 2 * LANES), 1)).astype(BF16)
     spread = jnp.concatenate([score] * (LANES // 8), axis=0)
     return total.astype(BF16), dot(unit, spread, 1, 1).astype(BF16)
@@ -183,11 +182,9 @@
 
 def back_kernel(hidden_ref, gate_ref, up_ref, place_ref, count_ref, out_ref, count_out):
     count_out[0, 0] = count_ref[0, 0]
-    width = gate_ref.shape[0]
-    rows, score = back_rows(hidden_ref, gate_ref, up_ref)
-    place = place_ref[:, : rows.shape[0]]
-    out_ref[:, :width] = dot(place, rows).astype(BF16)
-    out_ref[:, width:] = dot(place, score).astype(BF16)
+    rows = jnp.concatenate(back_rows(hidden_ref, gate_ref, up_ref), axis=1)
+    fill = jnp.zeros((place_ref.shape[1] - rows.shape[0], rows.shape[1]), BF16)
+    out_ref[...] = dot(place_ref[...], jnp.concatenate([rows, fill], axis=0)).astype(BF16)
 
 
 def rest_kernel(hidden_ref, gate_ref, up_ref, place_ref, main_ref, out_ref):
@@ -297,7 +294,7 @@
 
     def over_local(sums):
         sums = swap(sums, "local")
-        hidden = call(hidden_kernel, (parts, sums.shape[1] + EXTRA, 2 * LANES), sums)
+        hidden = call(hidden_kernel, (parts, sums.shape[1] + TAIL, 2 * LANES), sums)
         return swap(hidden, "local")
 
     hidden = over_local(main_sums)

time: 157 us -> 157 us (level)
  no operation moved by 1% of the time
where the time goes in v5:
time: 157 us; the launch traced here: 156 us
  blocking collectives  146 us (93%)
  Pallas kernels  8.9 us (6%)
    all_to_all x6, blocking collectives, swap(): lax.all_to_all(value, axis, split_axis=0, concat_axis=0, tiled=True, axis...  146 us

profile of v5, /device:TPU:8, one launch (start us, length us, event | category | flops | bytes accessed | tf_op | source)
XLA Modules:
  0.0 156.0 jit_solution(9576898580727599213)
XLA Ops:
  0.6 1.7 %shard_map.86 = bf16[8,16,1152]{2,1,0:T(8,128)(2,1)} custom-call(s32[8,16]{1,0:T(8,128)} %bitcast.18, f32[8,16]{1,0:T(8,128)} %bitcast.19, bf16[16,512]{1,0:T(8,128)(2,1)} %x_in.1, bf16[16,512]{1,0:T(8,128)(2,1)} %y_in.1), custom_call_target="tpu_custom_call" | custom-call | tf_op jit(solution)/shard_map/pallas_call | solution.py:261
  2.3 0.0 copy-start.1
  2.3 42.5 %all_to_all.39.tok_ref = bf16[8,16,1152]{2,1,0:T(8,128)(2,1)S(1)} all-to-all(bf16[8,16,1152]{2,1,0:T(8,128)(2,1)} %shard_map.86), channel_id=1, replica_groups={{0,128,256,384,512,640,768,896},{8,136,264,392,520,648,776,904},{16,144..., dimensions={0} | all-to-all | bytes 589824 | tf_op jit(solution)/shard_map/all_to_all | solution.py:247
  44.9 0.0 copy-start
  44.9 0.8 shard_map.87
  45.6 15.1 %all_to_all.40 = bf16[16,16,1024]{2,1,0:T(8,128)(2,1)S(1)} all-to-all(bf16[16,16,1024]{2,1,0:T(8,128)(2,1)S(1)} %shard_map.87), channel_id=1, replica_groups={{0,8,16,24,32,40,48,56,64,72,80,88,96,104,112,120},{128,136,144,152,160..., dimensions={0} | all-to-all | bytes 1048576 | tf_op jit(solution)/shard_map/all_to_all | solution.py:247
  60.7 0.0 copy-done.1
  60.7 0.0 copy-done
  60.7 2.6 %shard_map.88 = (bf16[8,160,384]{2,1,0:T(8,128)(2,1)S(1)}, bf16[8,96,384]{2,1,0:T(8,128)(2,1)S(1)}, bf16[256,256]{1,0:T(8,128)(2,1)S(1)}, s32[1,1]{1,0:T(1,128)}) custom-call(bf16[256,1024]{1,0:T(8,128)(2,1)S(1)} %bitcast.9, bf16[512,1024]{1,0:T(8,128)(2,1)S(1)} %bitcast.11, bf16[512,1024]{1,0:T(8,128)(2,1)} %bitcast.14, bf16[1024,512]{1,0:T(8,128)(2,1)S(1)} %bitcast.10), custom_call_target="tpu_custom_call" | custom-call | tf_op jit(solution)/shard_map/pallas_call | solution.py:277
  63.3 32.7 %all_to_all.41.parts_ref = bf16[8,160,384]{2,1,0:T(8,128)(2,1)S(1)} all-to-all(bf16[8,160,384]{2,1,0:T(8,128)(2,1)S(1)} %get-tuple-element.29), channel_id=1, replica_groups=mesh['node'=128,'local'=8] {'local'}, dimensions={0} | all-to-all | bytes 1966080 | tf_op jit(solution)/shard_map/all_to_all | solution.py:247
  96.0 0.4 shard_map.89
  96.4 0.0 copy-start.2
  96.4 21.9 %all_to_all.42.hidden_ref = bf16[8,168,256]{2,1,0:T(8,128)(2,1)S(1)} all-to-all(bf16[8,168,256]{2,1,0:T(8,128)(2,1)S(1)} %shard_map.89), channel_id=1, replica_groups=mesh['node'=128,'local'=8] {'local'}, dimensions={0} | all-to-all | bytes 1376256 | tf_op jit(solution)/shard_map/all_to_all | solution.py:247
  118.4 0.0 copy-done.2
  118.4 1.8 %shard_map.90 = (bf16[256,640]{1,0:T(8,128)(2,1)S(1)}, s32[1,1]{1,0:T(1,128)}) custom-call(bf16[8,168,256]{2,1,0:T(8,128)(2,1)S(1)} %all_to_all.42.hidden_ref, bf16[512,1024]{1,0:T(8,128)(2,1)S(1)} %bitcast.12, bf16[512,1024]{1,0:T(8,128)(2,1)S(1)} %bitcast.15, bf16[256,256]{1,0:T(8,128)(2,1)S(1)} %get-tuple-element.30.place_ref, ...), custom_call_target="tpu_custom_call" | custom-call | tf_op jit(solution)/shard_map/pallas_call | solution.py:301
  120.8 13.8 %all_to_all.43.back_ref = bf16[16,16,640]{2,1,0:T(8,128)(2,1)S(1)} all-to-all(bf16[16,16,640]{2,1,0:T(8,128)(2,1)S(1)} %bitcast.17), channel_id=1, replica_groups={{0,8,16,24,32,40,48,56,64,72,80,88,96,104,112,120},{128,136,144,152,160..., dimensions={0} | all-to-all | bytes 655360 | tf_op jit(solution)/shard_map/all_to_all | solution.py:247
  134.6 1.0 shard_map.91
  135.6 19.7 %all_to_all.44.parts_ref = bf16[8,16,640]{2,1,0:T(8,128)(2,1)S(1)} all-to-all(bf16[8,16,640]{2,1,0:T(8,128)(2,1)S(1)} %shard_map.91), channel_id=1, replica_groups={{0,128,256,384,512,640,768,896},{8,136,264,392,520,648,776,904},{16,144..., dimensions={0} | all-to-all | bytes 327680 | tf_op jit(solution)/shard_map/all_to_all | solution.py:247
  155.3 0.8 shard_map.92
  (1 shorter events, 0.0 us)
Async XLA Ops:
  2.3 58.4 %copy-start.1 = (bf16[1,512,1024]{2,1,0:T(8,128)(2,1)S(1)}, bf16[1,512,1024]{2,1,0:T(8,128)(2,1)}, u32[]{:S(2)}) copy-start(bf16[1,512,1024]{2,1,0:T(8,128)(2,1)} %param.13) | copy-start | bytes 3145732
  44.9 15.9 %copy-start = (bf16[1,1024,512]{2,1,0:T(8,128)(2,1)S(1)}, bf16[1,1024,512]{2,1,0:T(8,128)(2,1)}, u32[]{:S(2)}) copy-start(bf16[1,1024,512]{2,1,0:T(8,128)(2,1)} %param.15) | copy-start | bytes 3145732
  96.4 22.0 %copy-start.2 = (bf16[1,512,1024]{2,1,0:T(8,128)(2,1)S(1)}, bf16[1,512,1024]{2,1,0:T(8,128)(2,1)}, u32[]{:S(2)}) copy-start(bf16[1,512,1024]{2,1,0:T(8,128)(2,1)} %param.14) | copy-start | bytes 3145732

commit v6 on v5

--- a/solution.py
+++ b/solution.py
@@ -207,24 +207,31 @@
         value = sum(facts[:, i * routes + k : i * routes + k + 1] for i in (1, 2, 3))
         weight = jnp.where(hits[k], value, weight)
     sums = sum(dot(piece, back[:, :width]) for piece in split_three(weight))
-    lane = iota((groups * toks, LANES), 1)
-    scores = jnp.zeros((groups * toks, LANES), F32)
+    row = iota((TAIL, groups * toks), 0)
+    scores = jnp.zeros((TAIL, groups * toks), F32)
     for k in range(routes):
-        scores = jnp.where(lane == k, dot(hits[k].astype(BF16), back[:, width:]), scores)
-    out_ref[:, :, :width] = sums.astype(BF16).reshape(groups, toks, width)
-    out_ref[:, :, width:] = scores.astype(BF16).reshape(groups, toks, LANES)
+        found = dot(back[:, width:], hits[k].astype(BF16), 0, 1)
+        scores = jnp.where(row == k, found[:TAIL], scores)
+    sums = sums.astype(BF16)
+    for at in range(0, width, LANES):
+        place = at // LANES * toks
+        out_ref[:, place : place + toks, :] = sums[:, at : at + LANES].reshape(groups, toks, LANES)
+    for group in range(groups):
+        own = scores[:, group * toks : (group + 1) * toks]
+        own = jnp.concatenate([own, jnp.zeros((TAIL, LANES - toks), F32)], axis=1)
+        out_ref[group, width // LANES * toks :, :] = own.astype(BF16)
 
 
 def home_kernel(parts_ref, grad_ref, score_ref):
-    groups, toks, _ = parts_ref.shape
-    width = grad_ref.shape[1]
+    groups = parts_ref.shape[0]
+    toks, width = grad_ref.shape
     total = parts_ref[0].astype(F32)
     for group in range(1, groups):
         total += parts_ref[group].astype(F32)
-    grad_ref[...] = total[:, :width].astype(BF16)
-    unit = (iota((toks, toks), 0) == iota((toks, toks), 1)).astype(BF16)
-    scores = dot(total[:, width:].astype(BF16), unit, 0, 0)
-    score_ref[...] = scores[: score_ref.shape[0]].astype(BF16)
+    for at in range(0, width, LANES):
+        place = at // LANES * toks
+        grad_ref[:, at : at + LANES] = total[place : place + toks].astype(BF16)
+    score_ref[...] = total[width // LANES * toks :, :toks].astype(BF16)
 
 
 def on_device(hidden_in, grad_out, expert_ids, route_weights, gate_weight, up_weight, down_weight):
@@ -318,7 +325,7 @@
     back = swap(back.reshape(group_size, group_count * slot_cap, width + LANES), "node", within)
     home = call(
         functools.partial(combine_kernel, routes, slot_cap),
-        (group_count, tok_count, width + LANES), tokens, back,
+        (group_count, width // LANES * tok_count + TAIL, LANES), tokens, back,
     )
     home = swap(home, "node", across)
     grad_in, scores = call(home_kernel, [(tok_count, width), (routes, tok_count)], home)

time: 157 us -> 156 us (level)
  no operation moved by 1% of the time
where the time goes in v6:
time: 156 us; the launch traced here: 155 us
  blocking collectives  145 us (93%)
  Pallas kernels  8.78 us (6%)
    all_to_all x6, blocking collectives, swap(): lax.all_to_all(value, axis, split_axis=0, concat_axis=0, tiled=True, axis...  145 us

profile of v6, /device:TPU:8, one launch (start us, length us, event | category | flops | bytes accessed | tf_op | source)
XLA Modules:
  0.0 155.2 jit_solution(8868777508675349015)
XLA Ops:
  0.6 1.7 %shard_map.86 = bf16[8,16,1152]{2,1,0:T(8,128)(2,1)} custom-call(s32[8,16]{1,0:T(8,128)} %bitcast.18, f32[8,16]{1,0:T(8,128)} %bitcast.19, bf16[16,512]{1,0:T(8,128)(2,1)} %x_in.1, bf16[16,512]{1,0:T(8,128)(2,1)} %y_in.1), custom_call_target="tpu_custom_call" | custom-call | tf_op jit(solution)/shard_map/pallas_call | solution.py:268
  2.3 0.0 copy-start.1
  2.3 42.5 %all_to_all.39.tok_ref = bf16[8,16,1152]{2,1,0:T(8,128)(2,1)S(1)} all-to-all(bf16[8,16,1152]{2,1,0:T(8,128)(2,1)} %shard_map.86), channel_id=1, replica_groups={{0,128,256,384,512,640,768,896},{8,136,264,392,520,648,776,904},{16,144..., dimensions={0} | all-to-all | bytes 589824 | tf_op jit(solution)/shard_map/all_to_all | solution.py:254
  44.9 0.0 copy-start
  44.9 0.8 shard_map.87
  45.6 15.1 %all_to_all.40 = bf16[16,16,1024]{2,1,0:T(8,128)(2,1)S(1)} all-to-all(bf16[16,16,1024]{2,1,0:T(8,128)(2,1)S(1)} %shard_map.87), channel_id=1, replica_groups={{0,8,16,24,32,40,48,56,64,72,80,88,96,104,112,120},{128,136,144,152,160..., dimensions={0} | all-to-all | bytes 1048576 | tf_op jit(solution)/shard_map/all_to_all | solution.py:254
  60.7 0.0 copy-done.1
  60.7 0.0 copy-done
  60.7 2.6 %shard_map.88 = (bf16[8,160,384]{2,1,0:T(8,128)(2,1)S(1)}, bf16[8,96,384]{2,1,0:T(8,128)(2,1)S(1)}, bf16[256,256]{1,0:T(8,128)(2,1)S(1)}, s32[1,1]{1,0:T(1,128)}) custom-call(bf16[256,1024]{1,0:T(8,128)(2,1)S(1)} %bitcast.9, bf16[512,1024]{1,0:T(8,128)(2,1)S(1)} %bitcast.11, bf16[512,1024]{1,0:T(8,128)(2,1)} %bitcast.14, bf16[1024,512]{1,0:T(8,128)(2,1)S(1)} %bitcast.10), custom_call_target="tpu_custom_call" | custom-call | tf_op jit(solution)/shard_map/pallas_call | solution.py:284
  63.3 32.7 %all_to_all.41.parts_ref = bf16[8,160,384]{2,1,0:T(8,128)(2,1)S(1)} all-to-all(bf16[8,160,384]{2,1,0:T(8,128)(2,1)S(1)} %get-tuple-element.29), channel_id=1, replica_groups=mesh['node'=128,'local'=8] {'local'}, dimensions={0} | all-to-all | bytes 1966080 | tf_op jit(solution)/shard_map/all_to_all | solution.py:254
  96.0 0.4 shard_map.89
  96.4 0.0 copy-start.2
  96.4 21.9 %all_to_all.42.hidden_ref = bf16[8,168,256]{2,1,0:T(8,128)(2,1)S(1)} all-to-all(bf16[8,168,256]{2,1,0:T(8,128)(2,1)S(1)} %shard_map.89), channel_id=1, replica_groups=mesh['node'=128,'local'=8] {'local'}, dimensions={0} | all-to-all | bytes 1376256 | tf_op jit(solution)/shard_map/all_to_all | solution.py:254
  118.4 0.0 copy-done.2
  118.4 1.8 %shard_map.90 = (bf16[256,640]{1,0:T(8,128)(2,1)S(1)}, s32[1,1]{1,0:T(1,128)}) custom-call(bf16[8,168,256]{2,1,0:T(8,128)(2,1)S(1)} %all_to_all.42.hidden_ref, bf16[512,1024]{1,0:T(8,128)(2,1)S(1)} %bitcast.12, bf16[512,1024]{1,0:T(8,128)(2,1)S(1)} %bitcast.15, bf16[256,256]{1,0:T(8,128)(2,1)S(1)} %get-tuple-element.30.place_ref, ...), custom_call_target="tpu_custom_call" | custom-call | tf_op jit(solution)/shard_map/pallas_call | solution.py:308
  120.8 13.8 %all_to_all.43.back_ref = bf16[16,16,640]{2,1,0:T(8,128)(2,1)S(1)} all-to-all(bf16[16,16,640]{2,1,0:T(8,128)(2,1)S(1)} %bitcast.17), channel_id=1, replica_groups={{0,8,16,24,32,40,48,56,64,72,80,88,96,104,112,120},{128,136,144,152,160..., dimensions={0} | all-to-all | bytes 655360 | tf_op jit(solution)/shard_map/all_to_all | solution.py:254
  134.6 1.0 shard_map.91
  135.6 19.0 %all_to_all.44.parts_ref = bf16[8,72,128]{2,1,0:T(8,128)(2,1)S(1)} all-to-all(bf16[8,72,128]{2,1,0:T(8,128)(2,1)S(1)} %shard_map.91), channel_id=1, replica_groups={{0,128,256,384,512,640,768,896},{8,136,264,392,520,648,776,904},{16,144..., dimensions={0} | all-to-all | bytes 294912 | tf_op jit(solution)/shard_map/all_to_all | solution.py:254
  154.6 0.6 shard_map.92
  (1 shorter events, 0.0 us)
Async XLA Ops:
  2.3 58.4 %copy-start.1 = (bf16[1,512,1024]{2,1,0:T(8,128)(2,1)S(1)}, bf16[1,512,1024]{2,1,0:T(8,128)(2,1)}, u32[]{:S(2)}) copy-start(bf16[1,512,1024]{2,1,0:T(8,128)(2,1)} %param.13) | copy-start | bytes 3145732
  44.9 15.9 %copy-start = (bf16[1,1024,512]{2,1,0:T(8,128)(2,1)S(1)}, bf16[1,1024,512]{2,1,0:T(8,128)(2,1)}, u32[]{:S(2)}) copy-start(bf16[1,1024,512]{2,1,0:T(8,128)(2,1)} %param.15) | copy-start | bytes 3145732
  96.4 22.0 %copy-start.2 = (bf16[1,512,1024]{2,1,0:T(8,128)(2,1)S(1)}, bf16[1,512,1024]{2,1,0:T(8,128)(2,1)}, u32[]{:S(2)}) copy-start(bf16[1,512,1024]{2,1,0:T(8,128)(2,1)} %param.14) | copy-start | bytes 3145732

commit v7 on v6

--- a/solution.py
+++ b/solution.py
@@ -175,43 +175,73 @@
         total += dot(hidden_ref[j, :rows, :], weights, 1, 1)
         tails += hidden_ref[j, rows:, :].astype(F32)
     score = jnp.broadcast_to(tails[:1] + tails[4:5], tails.shape).astype(BF16)
-    unit = (iota((rows, 2 * LANES), 0) == iota((rows, 2 * LANES), 1)).astype(BF16)
-    spread = jnp.concatenate([score] * (LANES // 8), axis=0)
-    return total.astype(BF16), dot(unit, spread, 1, 1).astype(BF16)
+    return total.astype(BF16), score
+
+
+def put_back(moved, scores, out_ref):
+    places, _, _ = out_ref.shape
+    slots, width = moved.shape
+    each = slots // places
+    for at in range(0, width, LANES):
+        start = at // LANES * each
+        out_ref[:, start : start + each, :] = moved[:, at : at + LANES].astype(BF16).reshape(
+            places, each, LANES
+        )
+    for place in range(places):
+        own = scores[:, place * each : (place + 1) * each]
+        own = jnp.concatenate([own, jnp.zeros((TAIL, LANES - each), F32)], axis=1)
+        out_ref[place, width // LANES * each :, :] = own.astype(BF16)
+
+
+def read_back(back_ref, width):
+    places, height, _ = back_ref.shape
+    each = (height - TAIL) * LANES // width
+    pieces = [
+        back_ref[:, start : start + each, :].reshape(places * each, LANES)
+        for start in range(0, height - TAIL, each)
+    ]
+    tails = back_ref[:, height - TAIL :, :].astype(F32).reshape(places * TAIL, LANES)
+    shape = (LANES, places * each)
+    spread = dot(tails.astype(BF16), (iota(shape, 0) == iota(shape, 1) % each).astype(BF16))
+    row, column = iota(spread.shape, 0), iota(spread.shape, 1)
+    scores = jnp.sum(jnp.where(row == column // each * TAIL, spread, 0.0), axis=0, keepdims=True)
+    return jnp.concatenate(pieces, axis=1), jnp.broadcast_to(scores, (TAIL, scores.shape[1]))
 
 
 def back_kernel(hidden_ref, gate_ref, up_ref, place_ref, count_ref, out_ref, count_out):
     count_out[0, 0] = count_ref[0, 0]
-    rows = jnp.concatenate(back_rows(hidden_ref, gate_ref, up_ref), axis=1)
+    rows, score = back_rows(hidden_ref, gate_ref, up_ref)
     fill = jnp.zeros((place_ref.shape[1] - rows.shape[0], rows.shape[1]), BF16)
-    out_ref[...] = dot(place_ref[...], jnp.concatenate([rows, fill], axis=0)).astype(BF16)
+    moved = dot(place_ref[...], jnp.concatenate([rows, fill], axis=0))
+    put_back(moved, dot(score, place_ref[...], 1, 1), out_ref)
 
 
 def rest_kernel(hidden_ref, gate_ref, up_ref, place_ref, main_ref, out_ref):
-    width = gate_ref.shape[0]
     rows, score = back_rows(hidden_ref, gate_ref, up_ref)
-    place = place_ref[:, place_ref.shape[1] - rows.shape[0] :]
-    out_ref[:, :width] = (main_ref[:, :width].astype(F32) + dot(place, rows)).astype(BF16)
-    out_ref[:, width:] = (main_ref[:, width:].astype(F32) + dot(place, score)).astype(BF16)
+    last = place_ref[:, place_ref.shape[1] - rows.shape[0] :]
+    main, main_scores = read_back(main_ref, rows.shape[1])
+    moved = main.astype(F32) + dot(last, rows)
+    put_back(moved, main_scores + dot(score[:, : rows.shape[0]], last, 1, 1), out_ref)
 
 
 def combine_kernel(routes, slot_cap, tok_ref, back_ref, out_ref):
     groups, toks, full = tok_ref.shape
     size = back_ref.shape[0]
-    width = back_ref.shape[2] - LANES
+    width = (full - LANES) // 2
     facts = tok_ref[:, :, full - LANES :].reshape(groups * toks, LANES).astype(F32)
-    back = back_ref[...].reshape(size * groups * slot_cap, width + LANES)
+    back, slot_scores = read_back(back_ref, width)
+    slot_scores = slot_scores.astype(BF16)
     hits, _ = route_hits(facts, groups, toks, size, slot_cap, routes)
     weight = jnp.zeros(hits[0].shape, F32)
     for k in range(routes):
         value = sum(facts[:, i * routes + k : i * routes + k + 1] for i in (1, 2, 3))
         weight = jnp.where(hits[k], value, weight)
-    sums = sum(dot(piece, back[:, :width]) for piece in split_three(weight))
+    sums = sum(dot(piece, back) for piece in split_three(weight))
     row = iota((TAIL, groups * toks), 0)
     scores = jnp.zeros((TAIL, groups * toks), F32)
     for k in range(routes):
-        found = dot(back[:, width:], hits[k].astype(BF16), 0, 1)
-        scores = jnp.where(row == k, found[:TAIL], scores)
+        found = dot(slot_scores, hits[k].astype(BF16), 1, 1)
+        scores = jnp.where(row == k, found, scores)
     sums = sums.astype(BF16)
     for at in range(0, width, LANES):
         place = at // LANES * toks
@@ -305,10 +335,12 @@
         return swap(hidden, "local")
 
     hidden = over_local(main_sums)
+    each = group_count * slot_cap
+    back_shape = (group_size, width // LANES * each + TAIL, LANES)
     back, count = pl.pallas_call(
         back_kernel,
         out_shape=[
-            jax.ShapeDtypeStruct((slot_total, width + LANES), BF16),
+            jax.ShapeDtypeStruct(back_shape, BF16),
             jax.ShapeDtypeStruct((1, 1), jnp.int32),
         ],
         in_specs=[vmem, vmem, vmem, vmem, smem],
@@ -317,12 +349,12 @@
     )(hidden, w_gate, w_up, place, count)
 
     def add_rest(back, sums, place, w_gate, w_up):
-        return call(rest_kernel, (slot_total, width + LANES), over_local(sums), w_gate, w_up, place, back)
+        return call(rest_kernel, back_shape, over_local(sums), w_gate, w_up, place, back)
 
     back = lax.cond(
         count[0, 0] > main, add_rest, lambda back, *_: back, back, rest_sums, place, w_gate, w_up
     )
-    back = swap(back.reshape(group_size, group_count * slot_cap, width + LANES), "node", within)
+    back = swap(back, "node", within)
     home = call(
         functools.partial(combine_kernel, routes, slot_cap),
         (group_count, width // LANES * tok_count + TAIL, LANES), tokens, back,

time: 156 us -> 156 us (level)
  no operation moved by 1% of the time
where the time goes in v7:
time: 156 us; the launch traced here: 155 us
  blocking collectives  145 us (93%)
  Pallas kernels  8.83 us (6%)
    all_to_all x6, blocking collectives, swap(): lax.all_to_all(value, axis, split_axis=0, concat_axis=0, tiled=True, axis...  145 us

profile of v7, /device:TPU:8, one launch (start us, length us, event | category | flops | bytes accessed | tf_op | source)
XLA Modules:
  0.0 155.0 jit_solution(13904103810655349534)
XLA Ops:
  0.6 1.7 %shard_map.86 = bf16[8,16,1152]{2,1,0:T(8,128)(2,1)} custom-call(s32[8,16]{1,0:T(8,128)} %bitcast.16, f32[8,16]{1,0:T(8,128)} %bitcast.17, bf16[16,512]{1,0:T(8,128)(2,1)} %x_in.1, bf16[16,512]{1,0:T(8,128)(2,1)} %y_in.1), custom_call_target="tpu_custom_call" | custom-call | tf_op jit(solution)/shard_map/pallas_call | solution.py:298
  2.3 0.0 copy-start.1
  2.3 42.5 %all_to_all.39.tok_ref = bf16[8,16,1152]{2,1,0:T(8,128)(2,1)S(1)} all-to-all(bf16[8,16,1152]{2,1,0:T(8,128)(2,1)} %shard_map.86), channel_id=1, replica_groups={{0,128,256,384,512,640,768,896},{8,136,264,392,520,648,776,904},{16,144..., dimensions={0} | all-to-all | bytes 589824 | tf_op jit(solution)/shard_map/all_to_all | solution.py:284
  44.9 0.0 copy-start
  44.9 0.8 shard_map.87
  45.6 15.1 %all_to_all.40 = bf16[16,16,1024]{2,1,0:T(8,128)(2,1)S(1)} all-to-all(bf16[16,16,1024]{2,1,0:T(8,128)(2,1)S(1)} %shard_map.87), channel_id=1, replica_groups={{0,8,16,24,32,40,48,56,64,72,80,88,96,104,112,120},{128,136,144,152,160..., dimensions={0} | all-to-all | bytes 1048576 | tf_op jit(solution)/shard_map/all_to_all | solution.py:284
  60.7 0.0 copy-done.1
  60.7 0.0 copy-done
  60.7 2.6 %shard_map.88 = (bf16[8,160,384]{2,1,0:T(8,128)(2,1)S(1)}, bf16[8,96,384]{2,1,0:T(8,128)(2,1)S(1)}, bf16[256,256]{1,0:T(8,128)(2,1)S(1)}, s32[1,1]{1,0:T(1,128)}) custom-call(bf16[256,1024]{1,0:T(8,128)(2,1)S(1)} %bitcast.8, bf16[512,1024]{1,0:T(8,128)(2,1)S(1)} %bitcast.10, bf16[512,1024]{1,0:T(8,128)(2,1)} %bitcast.13, bf16[1024,512]{1,0:T(8,128)(2,1)S(1)} %bitcast.9), custom_call_target="tpu_custom_call" | custom-call | tf_op jit(solution)/shard_map/pallas_call | solution.py:314
  63.3 32.7 %all_to_all.41.parts_ref = bf16[8,160,384]{2,1,0:T(8,128)(2,1)S(1)} all-to-all(bf16[8,160,384]{2,1,0:T(8,128)(2,1)S(1)} %get-tuple-element.29), channel_id=1, replica_groups=mesh['node'=128,'local'=8] {'local'}, dimensions={0} | all-to-all | bytes 1966080 | tf_op jit(solution)/shard_map/all_to_all | solution.py:284
  96.0 0.4 shard_map.89
  96.4 0.0 copy-start.2
  96.4 21.9 %all_to_all.42.hidden_ref = bf16[8,168,256]{2,1,0:T(8,128)(2,1)S(1)} all-to-all(bf16[8,168,256]{2,1,0:T(8,128)(2,1)S(1)} %shard_map.89), channel_id=1, replica_groups=mesh['node'=128,'local'=8] {'local'}, dimensions={0} | all-to-all | bytes 1376256 | tf_op jit(solution)/shard_map/all_to_all | solution.py:284
  118.4 0.0 copy-done.2
  118.4 1.8 %shard_map.90 = (bf16[16,72,128]{2,1,0:T(8,128)(2,1)S(1)}, s32[1,1]{1,0:T(1,128)}) custom-call(bf16[8,168,256]{2,1,0:T(8,128)(2,1)S(1)} %all_to_all.42.hidden_ref, bf16[512,1024]{1,0:T(8,128)(2,1)S(1)} %bitcast.11, bf16[512,1024]{1,0:T(8,128)(2,1)S(1)} %bitcast.14, bf16[256,256]{1,0:T(8,128)(2,1)S(1)} %get-tuple-element.30.place_ref, ...), custom_call_target="tpu_custom_call" | custom-call | tf_op jit(solution)/shard_map/pallas_call | solution.py:340
  120.8 13.5 %all_to_all.43.back_ref = bf16[16,72,128]{2,1,0:T(8,128)(2,1)S(1)} all-to-all(bf16[16,72,128]{2,1,0:T(8,128)(2,1)S(1)} %get-tuple-element.37), channel_id=1, replica_groups={{0,8,16,24,32,40,48,56,64,72,80,88,96,104,112,120},{128,136,144,152,160..., dimensions={0} | all-to-all | bytes 589824 | tf_op jit(solution)/shard_map/all_to_all | solution.py:284
  134.3 1.0 shard_map.91
  135.3 19.0 %all_to_all.44.parts_ref = bf16[8,72,128]{2,1,0:T(8,128)(2,1)S(1)} all-to-all(bf16[8,72,128]{2,1,0:T(8,128)(2,1)S(1)} %shard_map.91), channel_id=1, replica_groups={{0,128,256,384,512,640,768,896},{8,136,264,392,520,648,776,904},{16,144..., dimensions={0} | all-to-all | bytes 294912 | tf_op jit(solution)/shard_map/all_to_all | solution.py:284
  154.4 0.6 shard_map.92
  (1 shorter events, 0.0 us)
Async XLA Ops:
  2.3 58.4 %copy-start.1 = (bf16[1,512,1024]{2,1,0:T(8,128)(2,1)S(1)}, bf16[1,512,1024]{2,1,0:T(8,128)(2,1)}, u32[]{:S(2)}) copy-start(bf16[1,512,1024]{2,1,0:T(8,128)(2,1)} %param.13) | copy-start | bytes 3145732
  44.9 15.9 %copy-start = (bf16[1,1024,512]{2,1,0:T(8,128)(2,1)S(1)}, bf16[1,1024,512]{2,1,0:T(8,128)(2,1)}, u32[]{:S(2)}) copy-start(bf16[1,1024,512]{2,1,0:T(8,128)(2,1)} %param.15) | copy-start | bytes 3145732
  96.4 22.0 %copy-start.2 = (bf16[1,512,1024]{2,1,0:T(8,128)(2,1)S(1)}, bf16[1,512,1024]{2,1,0:T(8,128)(2,1)}, u32[]{:S(2)}) copy-start(bf16[1,512,1024]{2,1,0:T(8,128)(2,1)} %param.14) | copy-start | bytes 3145732

commit v8 on v6

--- a/solution.py
+++ b/solution.py
@@ -38,20 +38,23 @@
     copies = [pltpu.make_async_copy(*pair, sems.at[i]) for i, pair in enumerate(pairs)]
     for copy in copies:
         copy.start()
-    for copy in copies:
-        copy.wait()
     groups, toks, _ = out_ref.shape
     routes = ids_ref.shape[0]
     width = x_ref.shape[1]
     unit = (iota((toks, toks), 0) == iota((toks, toks), 1)).astype(BF16)
+    copies[0].wait()
+    copies[1].wait()
     pieces = [piece.astype(F32) for piece in split_three(route_ref[...])]
     fill = jnp.zeros((LANES - 4 * routes, toks), F32)
+    facts = jnp.concatenate([ids_ref[...].astype(F32), *pieces, fill], axis=0).astype(BF16)
+    facts = dot(unit, facts, 1, 1)
+    names = iota(facts.shape, 1) < routes
+    copies[2].wait()
+    copies[3].wait()
     for group in range(groups):
-        ids = (ids_ref[...] - group * size).astype(F32)
-        facts = jnp.concatenate([ids, *pieces, fill], axis=0).astype(BF16)
         out_ref[group, :, :width] = x_ref[...]
         out_ref[group, :, width : 2 * width] = y_ref[...]
-        out_ref[group, :, 2 * width :] = dot(unit, facts, 1, 1).astype(BF16)
+        out_ref[group, :, 2 * width :] = jnp.where(names, facts - group * size, facts).astype(BF16)
 
 
 def route_hits(facts, groups, toks, size, slot_cap, routes):

time: 156 us -> 156 us (level)
  no operation moved by 1% of the time
where the time goes in v8:
time: 156 us; the launch traced here: 155 us
  blocking collectives  145 us (93%)
  Pallas kernels  8.7 us (6%)
    all_to_all x6, blocking collectives, swap(): lax.all_to_all(value, axis, split_axis=0, concat_axis=0, tiled=True, axis...  145 us

profile of v8, /device:TPU:8, one launch (start us, length us, event | category | flops | bytes accessed | tf_op | source)
XLA Modules:
  0.0 155.2 jit_solution(11400455677553569321)
XLA Ops:
  0.6 1.6 %shard_map.86 = bf16[8,16,1152]{2,1,0:T(8,128)(2,1)} custom-call(s32[8,16]{1,0:T(8,128)} %bitcast.18, f32[8,16]{1,0:T(8,128)} %bitcast.19, bf16[16,512]{1,0:T(8,128)(2,1)} %x_in.1, bf16[16,512]{1,0:T(8,128)(2,1)} %y_in.1), custom_call_target="tpu_custom_call" | custom-call | tf_op jit(solution)/shard_map/pallas_call | solution.py:271
  2.2 0.0 copy-start.1
  2.3 42.5 %all_to_all.39.tok_ref = bf16[8,16,1152]{2,1,0:T(8,128)(2,1)S(1)} all-to-all(bf16[8,16,1152]{2,1,0:T(8,128)(2,1)} %shard_map.86), channel_id=1, replica_groups={{0,128,256,384,512,640,768,896},{8,136,264,392,520,648,776,904},{16,144..., dimensions={0} | all-to-all | bytes 589824 | tf_op jit(solution)/shard_map/all_to_all | solution.py:257
  44.8 0.0 copy-start
  44.8 0.8 shard_map.87
  45.6 15.1 %all_to_all.40 = bf16[16,16,1024]{2,1,0:T(8,128)(2,1)S(1)} all-to-all(bf16[16,16,1024]{2,1,0:T(8,128)(2,1)S(1)} %shard_map.87), channel_id=1, replica_groups={{0,8,16,24,32,40,48,56,64,72,80,88,96,104,112,120},{128,136,144,152,160..., dimensions={0} | all-to-all | bytes 1048576 | tf_op jit(solution)/shard_map/all_to_all | solution.py:257
  60.6 0.0 copy-done.1
  60.6 0.0 copy-done
  60.6 2.6 %shard_map.88 = (bf16[8,160,384]{2,1,0:T(8,128)(2,1)S(1)}, bf16[8,96,384]{2,1,0:T(8,128)(2,1)S(1)}, bf16[256,256]{1,0:T(8,128)(2,1)S(1)}, s32[1,1]{1,0:T(1,128)}) custom-call(bf16[256,1024]{1,0:T(8,128)(2,1)S(1)} %bitcast.9, bf16[512,1024]{1,0:T(8,128)(2,1)S(1)} %bitcast.11, bf16[512,1024]{1,0:T(8,128)(2,1)} %bitcast.14, bf16[1024,512]{1,0:T(8,128)(2,1)S(1)} %bitcast.10), custom_call_target="tpu_custom_call" | custom-call | tf_op jit(solution)/shard_map/pallas_call | solution.py:287
  63.2 32.7 %all_to_all.41.parts_ref = bf16[8,160,384]{2,1,0:T(8,128)(2,1)S(1)} all-to-all(bf16[8,160,384]{2,1,0:T(8,128)(2,1)S(1)} %get-tuple-element.29), channel_id=1, replica_groups=mesh['node'=128,'local'=8] {'local'}, dimensions={0} | all-to-all | bytes 1966080 | tf_op jit(solution)/shard_map/all_to_all | solution.py:257
  96.0 0.4 shard_map.89
  96.3 0.0 copy-start.2
  96.3 21.9 %all_to_all.42.hidden_ref = bf16[8,168,256]{2,1,0:T(8,128)(2,1)S(1)} all-to-all(bf16[8,168,256]{2,1,0:T(8,128)(2,1)S(1)} %shard_map.89), channel_id=1, replica_groups=mesh['node'=128,'local'=8] {'local'}, dimensions={0} | all-to-all | bytes 1376256 | tf_op jit(solution)/shard_map/all_to_all | solution.py:257
  118.3 0.0 copy-done.2
  118.3 1.8 %shard_map.90 = (bf16[256,640]{1,0:T(8,128)(2,1)S(1)}, s32[1,1]{1,0:T(1,128)}) custom-call(bf16[8,168,256]{2,1,0:T(8,128)(2,1)S(1)} %all_to_all.42.hidden_ref, bf16[512,1024]{1,0:T(8,128)(2,1)S(1)} %bitcast.12, bf16[512,1024]{1,0:T(8,128)(2,1)S(1)} %bitcast.15, bf16[256,256]{1,0:T(8,128)(2,1)S(1)} %get-tuple-element.30.place_ref, ...), custom_call_target="tpu_custom_call" | custom-call | tf_op jit(solution)/shard_map/pallas_call | solution.py:311
  120.7 13.8 %all_to_all.43.back_ref = bf16[16,16,640]{2,1,0:T(8,128)(2,1)S(1)} all-to-all(bf16[16,16,640]{2,1,0:T(8,128)(2,1)S(1)} %bitcast.17), channel_id=1, replica_groups={{0,8,16,24,32,40,48,56,64,72,80,88,96,104,112,120},{128,136,144,152,160..., dimensions={0} | all-to-all | bytes 655360 | tf_op jit(solution)/shard_map/all_to_all | solution.py:257
  134.5 1.0 shard_map.91
  135.5 19.0 %all_to_all.44.parts_ref = bf16[8,72,128]{2,1,0:T(8,128)(2,1)S(1)} all-to-all(bf16[8,72,128]{2,1,0:T(8,128)(2,1)S(1)} %shard_map.91), channel_id=1, replica_groups={{0,128,256,384,512,640,768,896},{8,136,264,392,520,648,776,904},{16,144..., dimensions={0} | all-to-all | bytes 294912 | tf_op jit(solution)/shard_map/all_to_all | solution.py:257
  154.5 0.6 shard_map.92
  (1 shorter events, 0.0 us)
Async XLA Ops:
  2.2 58.4 %copy-start.1 = (bf16[1,512,1024]{2,1,0:T(8,128)(2,1)S(1)}, bf16[1,512,1024]{2,1,0:T(8,128)(2,1)}, u32[]{:S(2)}) copy-start(bf16[1,512,1024]{2,1,0:T(8,128)(2,1)} %param.13) | copy-start | bytes 3145732
  44.8 15.9 %copy-start = (bf16[1,1024,512]{2,1,0:T(8,128)(2,1)S(1)}, bf16[1,1024,512]{2,1,0:T(8,128)(2,1)}, u32[]{:S(2)}) copy-start(bf16[1,1024,512]{2,1,0:T(8,128)(2,1)} %param.15) | copy-start | bytes 3145732
  96.3 22.0 %copy-start.2 = (bf16[1,512,1024]{2,1,0:T(8,128)(2,1)S(1)}, bf16[1,512,1024]{2,1,0:T(8,128)(2,1)}, u32[]{:S(2)}) copy-start(bf16[1,512,1024]{2,1,0:T(8,128)(2,1)} %param.14) | copy-start | bytes 3145732
